TPU v7x, 32 devices: a whole 2x2x4 slice. The times are simulated.
32 devices in a mesh: group: 2 (over y), expert: 4 (over z), tensor: 4 (over x, core).
Axes of the slice: x: 2, y: 2, z: 4, core: 2. Of those that a mesh axis runs over, the one named last changes fastest.
Arguments:
- stream: bfloat16 [2, 8, 384, 4096], P(None, ('group', 'expert'), 'tensor'), parts along dimension 1, may hold values from -6 to 6
- queries: bfloat16 [2, 8, 384, 4096], P(None, ('group', 'expert'), None, 'tensor'), parts along dimension 1, may hold values from -160 to 160
- key_rows: bfloat16 [2, 8, 384, 256], P(None, ('group', 'expert'), 'tensor'), parts along dimension 1, may hold values from -4 to 4
- value_rows: bfloat16 [2, 8, 384, 256], P(None, ('group', 'expert'), 'tensor'), parts along dimension 1, may hold values from -6 to 6
- segments: int32 [2, 8, 384], P(None, ('group', 'expert')), parts along dimension 1, may hold values from 0 to 1, never falling along the last dimension, each value on 1 to 288 neighbouring positions
- out_proj: bfloat16 [4096, 4096], P('tensor', 'expert'), may hold values from -0.09375 to 0.09375
- norm_gain: float32 [4096], replicated, may hold values from 0.1 to 1.9
- router: bfloat16 [4096, 8], replicated, may hold values from -0.09375 to 0.09375
- routes: int32 [2, 8, 384, 2], P(None, ('group', 'expert'), 'tensor'), parts along dimension 1, may hold values from 0 to 7, all different within a row; in each aligned block of 96 rows (0 to 95, 96 to 191, ..., all dimensions but the last counted through in order) at most 36 rows name the same one
- gate_proj: bfloat16 [16, 4096, 384], P(('expert', 'tensor')), may hold values from -0.09375 to 0.09375
- up_proj: bfloat16 [16, 4096, 384], P(('expert', 'tensor')), may hold values from -0.09375 to 0.09375
- down_proj: bfloat16 [16, 384, 4096], P(('expert', 'tensor')), may hold values from -0.21875 to 0.21875
Outputs:
- layer_out: bfloat16 [2, 8, 384, 4096], P(None, ('group', 'expert'), 'tensor'), parts along dimension 1
There are 2 independent parts, one for each index of `group`. A program takes and returns all parts, laid end to end along the dimension named above; an argument that names none is the same for every part. Nothing has to cross between parts.
Inputs may be any that keep to these rules, and one draw needn't show every extreme that they name: `routes`: each row names 2 different experts. Within the rows of one device in one micro-batch (aligned blocks of 96 rows) no expert is named more than 36 times, a bound that some block reaches. `segments`: within each micro-batch of a request group the document numbers never fall; each document holds 1 to 288 tokens.
All inputs are finite; a program needn't handle non-finite values.
Results may differ from a plain program's by a relative error of at most 0.0095.
Values may be sent and summed in bfloat16 or wider, within the bound.
A program may use at most 128 MiB of HBM per device.

v0:
```python
import math

import jax
import jax.numpy as jnp
from jax import lax
from jax.sharding import PartitionSpec as P

HEADS = 32
KV = 2
HD = 128
TOPK = 2


epsilon = 1e-06


def attend_rows(query_block, key_all, value_all, segment_ids, kv_head):
    seq_rows = key_all.shape[0]
    heads_here = query_block.shape[-1] // HD
    key_head = lax.dynamic_slice_in_dim(key_all, kv_head * HD, HD, 1)
    value_head = lax.dynamic_slice_in_dim(value_all, kv_head * HD, HD, 1)
    query_heads = query_block.reshape(seq_rows, heads_here, HD)
    scores = jnp.einsum(
        "qhd,kd->hqk", query_heads, key_head, preferred_element_type=jnp.float32
    ) * (1.0 / math.sqrt(HD))
    positions = lax.broadcasted_iota(jnp.int32, (seq_rows, seq_rows), 0)
    columns = lax.broadcasted_iota(jnp.int32, (seq_rows, seq_rows), 1)
    allowed = (segment_ids[:, None] == segment_ids[None, :]) & (columns <= positions)
    masked = jnp.where(allowed[None], scores, -1e30)
    largest = jnp.max(masked, axis=-1, keepdims=True)
    powered = jnp.where(allowed[None], jnp.exp(masked - largest), 0.0)
    probs = (powered / jnp.sum(powered, axis=-1, keepdims=True)).astype(jnp.bfloat16)
    attended = jnp.einsum("hqk,kd->qhd", probs, value_head, preferred_element_type=jnp.float32)
    return attended.astype(jnp.bfloat16).reshape(seq_rows, heads_here * HD)


def expert_rows(rows_in, gate_w, up_w, down_w):
    flat_rows = rows_in.reshape(-1, rows_in.shape[-1])
    gate_val = jnp.dot(flat_rows, gate_w, preferred_element_type=jnp.float32)
    up_val = jnp.dot(flat_rows, up_w, preferred_element_type=jnp.float32)
    hidden = (jax.nn.silu(gate_val) * up_val).astype(jnp.bfloat16)
    result = jnp.dot(hidden, down_w, preferred_element_type=jnp.float32).astype(jnp.bfloat16)
    return result.reshape(rows_in.shape)


def local(
    stream,
    queries,
    key_rows,
    value_rows,
    segments,
    out_proj,
    norm_gain,
    router,
    routes,
    gate_proj,
    up_proj,
    down_proj,
):
    tensor_index = lax.axis_index("tensor")
    heads_here = queries.shape[-1] // HD
    kv_head = tensor_index * heads_here // (HEADS // KV)
    proj_full = lax.all_gather(out_proj, "expert", axis=1, tiled=True)
    tok_rows = stream.shape[2]
    model_width = stream.shape[3]
    n_experts = router.shape[1]
    capacity = max(2, 3 * tok_rows * TOPK // (2 * n_experts))
    gate_w = gate_proj[0]
    up_w = up_proj[0]
    down_w = down_proj[0]
    results = []
    for micro in range(stream.shape[0]):
        key_all, value_all = (
            lax.all_gather(key_rows[micro, 0], "tensor", axis=0, tiled=True),
            lax.all_gather(value_rows[micro, 0], "tensor", axis=0, tiled=True),
        )
        attended = attend_rows(queries[micro, 0], key_all, value_all, segments[micro, 0], kv_head)

        def project(begin_row, row_count, attended=attended):
            return jnp.dot(attended, proj_full, preferred_element_type=jnp.float32)

        attn_out = lax.psum_scatter(
            project(jnp.int32(0), tok_rows * lax.axis_size("tensor")).astype(jnp.bfloat16),
            "tensor",
            scatter_dimension=0,
            tiled=True,
        ).astype(jnp.float32)
        residual = stream[micro, 0].astype(jnp.float32) + attn_out
        scale = lax.rsqrt(jnp.mean(residual * residual, axis=-1, keepdims=True) + epsilon)
        normed = (residual * scale * norm_gain).astype(jnp.bfloat16)
        logits = jnp.dot(normed, router, preferred_element_type=jnp.float32)
        chosen = routes[micro, 0]
        expert_iota = lax.broadcasted_iota(jnp.int32, (1, 1, n_experts), 2)
        picks = chosen[:, :, None] == expert_iota
        picked = jnp.sum(jnp.where(picks, logits[:, None, :], 0.0), axis=-1)
        mixing = 1.0 / jnp.sum(jnp.exp(picked[:, None, :] - picked[:, :, None]), axis=-1)
        copy_hot = picks.reshape(tok_rows * TOPK, n_experts).astype(jnp.int32)
        earlier = jnp.cumsum(copy_hot, axis=0) - copy_hot
        slot_of = jnp.sum(earlier * copy_hot, axis=-1).reshape(tok_rows, TOPK)
        position = chosen * capacity + slot_of
        slot_iota = lax.broadcasted_iota(jnp.int32, (1, 1, n_experts * capacity), 2)
        placing = jnp.sum((position[:, :, None] == slot_iota).astype(jnp.bfloat16), axis=1)
        packed = jnp.einsum(
            "tc,td->cd", placing, normed, preferred_element_type=jnp.float32
        ).astype(jnp.bfloat16)
        packed = packed.reshape(n_experts, 1, capacity, model_width)
        outgoing = jnp.broadcast_to(packed, (n_experts, 2, capacity, model_width)).reshape(
            2 * n_experts, capacity, model_width
        )
        returned = lax.all_to_all(
            expert_rows(
                lax.all_to_all(
                    outgoing, ("expert", "tensor"), split_axis=0, concat_axis=0, tiled=True
                ),
                gate_w,
                up_w,
                down_w,
            ),
            ("expert", "tensor"),
            split_axis=0,
            concat_axis=0,
            tiled=True,
        )
        halves = returned.reshape(n_experts, 2, capacity, model_width).astype(jnp.float32)
        expert_out = (
            (halves[:, 0] + halves[:, 1])
            .astype(jnp.bfloat16)
            .reshape(n_experts * capacity, model_width)
        )
        fetched = jnp.take(expert_out, position.reshape(-1), axis=0).reshape(
            tok_rows, TOPK, model_width
        )
        mixed = residual + jnp.sum(mixing[:, :, None] * fetched.astype(jnp.float32), axis=1)
        results.append(mixed.astype(jnp.bfloat16))
    return jnp.stack(results)[:, None]


def solution(mesh):
    return jax.shard_map(
        local,
        mesh=mesh,
        in_specs=(
            P(None, ("group", "expert"), "tensor", None),
            P(None, ("group", "expert"), None, "tensor"),
            P(None, ("group", "expert"), "tensor", None),
            P(None, ("group", "expert"), "tensor", None),
            P(None, ("group", "expert"), None),
            P("tensor", "expert"),
            P(),
            P(),
            P(None, ("group", "expert"), "tensor", None),
            P(("expert", "tensor"), None, None),
            P(("expert", "tensor"), None, None),
            P(("expert", "tensor"), None, None),
        ),
        out_specs=P(None, ("group", "expert"), "tensor", None),
        check_vma=False,
    )
```

profile of v0, /device:TPU:11, one launch (start us, length us, event | category | flops | bytes accessed | tf_op | source)
XLA Modules:
  0.0 786.2 jit_solution(8951246155288012879)
XLA Ops:
  6.5 0.7 all-gather.6.cloned.1.call-update
  7.3 2.8 fusion.104
  10.1 2.3 copy.74
  12.4 0.6 fusion.106
  13.1 6.1 all-gather.3
  19.2 0.6 fusion.105
  19.8 5.6 all-gather.2
  25.4 0.8 fusion.46
  26.2 5.4 fusion.113
  31.6 3.9 fusion.26
  35.5 121.5 %all-gather.6.cloned.1.call-done = bf16[1024,4096]{1,0:T(8,128)(2,1)} async-done(((bf16[1024,1024]{1,0:T(8,128)(2,1)}), bf16[1024,4096]{1,0:T(8,128)(2,1)}) %all-gather.6.cloned.1.call-update) | async-done | bytes 8388624 | tf_op jit(solution)/shard_map/all_gather | solution.py:63
  157.0 8.8 %convolution_convert_fusion.2 = bf16[384,4096]{1,0:T(8,128)(2,1)} fusion(bf16[384,1024]{0,1:T(8,128)(2,1)} %bitcast.193, bf16[1024,4096]{1,0:T(8,128)(2,1)} %all-gather.6.cloned.1.call-done), kind=kOutput, calls=%fused_computation.6 | convolution fusion | flops 3222798336 | bytes 12320768 | tf_op jit(solution)/shard_map/dot_general | solution.py:80
  165.8 2.3 copy.70
  168.2 6.1 all-gather.1
  174.3 6.3 all-gather
  180.5 0.8 fusion.47
  181.3 5.4 fusion.108
  186.7 2.9 fusion.27
  189.7 8.7 %convolution_convert_fusion.3 = bf16[384,4096]{1,0:T(8,128)(2,1)} fusion(bf16[384,1024]{0,1:T(8,128)(2,1)S(1)} %bitcast.194, bf16[1024,4096]{1,0:T(8,128)(2,1)} %all-gather.6.cloned.1.call-done), kind=kOutput, calls=%fused_computation.7 | convolution fusion | flops 3222798336 | bytes 12320768 | tf_op jit(solution)/shard_map/dot_general | solution.py:80
  198.4 0.7 copy-done.19
  199.3 0.6 reduce-window.16
  200.6 3.3 reduce-scatter.5.cloned.1.call-done
  203.9 40.7 %reduce-scatter.3.cloned.1.call-done = bf16[96,4096]{1,0:T(8,128)(2,1)} async-done(((bf16[384,4096]{1,0:T(8,128)(2,1)}), bf16[96,4096]{1,0:T(8,128)(2,1)}) %reduce-scatter.3.cloned.1.call-update) | async-done | bytes 786448 | tf_op jit(solution)/shard_map/reduce_scatter | solution.py:82
  244.6 2.6 multiply_reduce_fusion.3
  247.4 1.6 multiply_convert_fusion.1
  248.9 0.9 copy-done.7
  249.8 2.2 convolution_convert_fusion.4
  252.1 4.1 broadcast_in_dim.103
  256.2 4.7 broadcast_in_dim.104
  260.9 6.4 all-to-all-start.2
  268.9 3.3 convolution_convert_fusion.5
  272.2 4.1 broadcast_in_dim.99
  276.3 105.9 %all-to-all-done.2 = bf16[16,36,4096]{2,1,0:T(8,128)(2,1)} async-done(((bf16[16,36,4096]{2,1,0:T(8,128)(2,1)}), bf16[16,36,4096]{2,1,0:T(8,128)(2,1)}, u32[]{:S(2)}, u32[]{:S(2)}) %all-to-all-start.2) | async-done | bytes 4718624 | tf_op jit(solution)/shard_map/all_to_all | solution.py:112
  382.2 4.6 broadcast_in_dim.100
  386.9 5.2 all-to-all-start
  392.1 7.3 reshape.243
  399.4 6.8 fusion.14
  406.3 10.6 %convolution_convert_fusion = bf16[576,4096]{1,0:T(8,128)(2,1)} fusion(bf16[1,384,4096]{2,1,0:T(8,128)(2,1)S(1)} %copy-done, bf16[576,4096]{1,0:T(8,128)(2,1)} %reshape.243, bf16[1,4096,384]{2,1,0:T(8,128)(2,1)} %param.24, f32[576,384]{1,0:T(8,128)} %fusion.14), kind=kOutput, calls=%fused_computation.4 | convolution fusion | flops 3627565056 | bytes 16613376 | tf_op jit(solution)/shard_map/dot_general | solution.py:42
  416.9 7.3 reshape.244
  424.2 82.8 %all-to-all-done = bf16[16,36,4096]{2,1,0:T(8,128)(2,1)} async-done(((bf16[16,36,4096]{2,1,0:T(8,128)(2,1)}), bf16[16,36,4096]{2,1,0:T(8,128)(2,1)}, u32[]{:S(2)}, u32[]{:S(2)}) %all-to-all-start) | async-done | bytes 4718624 | tf_op jit(solution)/shard_map/all_to_all | solution.py:112
  506.9 4.9 all-to-all-start.3
  511.8 7.3 reshape.236
  519.1 6.8 fusion.16
  525.9 10.6 %convolution_convert_fusion.1 = bf16[576,4096]{1,0:T(8,128)(2,1)} fusion(bf16[1,384,4096]{2,1,0:T(8,128)(2,1)S(1)} %copy-done, bf16[576,4096]{1,0:T(8,128)(2,1)} %reshape.236, bf16[1,4096,384]{2,1,0:T(8,128)(2,1)} %param.24, f32[576,384]{1,0:T(8,128)} %fusion.16), kind=kOutput, calls=%fused_computation.5 | convolution fusion | flops 3627565056 | bytes 16613376 | tf_op jit(solution)/shard_map/dot_general | solution.py:42
  536.5 7.2 reshape.237
  543.8 82.9 %all-to-all-done.3 = bf16[16,36,4096]{2,1,0:T(8,128)(2,1)} async-done(((bf16[16,36,4096]{2,1,0:T(8,128)(2,1)}), bf16[16,36,4096]{2,1,0:T(8,128)(2,1)}, u32[]{:S(2)}, u32[]{:S(2)}) %all-to-all-start.3) | async-done | bytes 4718624 | tf_op jit(solution)/shard_map/all_to_all | solution.py:110
  626.7 5.3 all-to-all-start.1
  633.2 3.9 convert.23
  637.1 2.2 fusion.3
  639.3 2.7 convert_element_type.164
  642.0 2.7 gather_fusion.1
  644.7 1.7 select_convert_fusion
  646.3 3.2 reshape.252
  649.6 97.2 %all-to-all-done.1 = bf16[16,36,4096]{2,1,0:T(8,128)(2,1)} async-done(((bf16[16,36,4096]{2,1,0:T(8,128)(2,1)}), bf16[16,36,4096]{2,1,0:T(8,128)(2,1)}, u32[]{:S(2)}, u32[]{:S(2)}) %all-to-all-start.1) | async-done | bytes 4718624 | tf_op jit(solution)/shard_map/all_to_all | solution.py:110
  746.8 3.9 convert.22
  750.7 2.2 fusion.5
  752.9 2.7 convert_element_type.144
  755.6 2.7 gather_fusion
  758.3 3.4 select_convert_fusion.1
  761.7 5.6 reshape.248
  767.3 4.8 multiply_reduce_fusion
  772.1 4.9 multiply_reduce_fusion.1
  777.1 0.7 fusion.40
  777.8 1.3 maximum_bitcast_fusion
  (88 shorter events, 4.1 us)
Async XLA Ops:
  6.5 399.7 %copy-start = (bf16[1,384,4096]{2,1,0:T(8,128)(2,1)S(1)}, bf16[1,384,4096]{2,1,0:T(8,128)(2,1)}, u32[]{:S(2)}) copy-start(bf16[1,384,4096]{2,1,0:T(8,128)(2,1)} %param.25) | copy-start | bytes 9437188
  6.5 5.9 copy-start.15
  6.5 12.6 %copy-start.16 = (bf16[2,1,96,256]{3,2,1,0:T(8,128)(2,1)S(1)}, bf16[2,1,96,256]{3,2,1,0:T(8,128)(2,1)}, u32[]{:S(2)}) copy-start(bf16[2,1,96,256]{3,2,1,0:T(8,128)(2,1)} %param.17) | copy-start | bytes 294916
  6.5 150.5 %all-gather.6.cloned.1.call-start = ((), (), s32[]{:S(2)}) async-start(), calls=%async_computation.6 | async-start | bytes 10485760 | tf_op jit(solution)/shard_map/all_gather | solution.py:63
  7.3 18.1 %copy-start.18 = (s32[2,1,384]{2,1,0:T(1,128)S(1)}, s32[2,1,384]{2,1,0:T(1,128)}, u32[]{:S(2)}) copy-start(s32[2,1,384]{2,1,0:T(1,128)} %param.18) | copy-start | bytes 9220
  7.3 196.6 %reduce-scatter.5.cloned.1.call-start = ((), (), s32[]{:S(2)}) async-start(), calls=%async_computation.8 | async-start | bytes 3932160 | tf_op jit(solution)/shard_map/reduce_scatter | solution.py:82
  165.8 2.4 copy-start.14
  165.8 78.8 %reduce-scatter.3.cloned.1.call-start = ((), (), s32[]{:S(2)}) async-start(), calls=%async_computation.7 | async-start | bytes 3932160 | tf_op jit(solution)/shard_map/reduce_scatter | solution.py:82
  198.4 0.7 copy-start.19
  198.4 48.9 %copy-start.17 = (f32[4096]{0:T(1024)S(1)}, f32[4096]{0:T(1024)}, u32[]{:S(2)}) copy-start(f32[4096]{0:T(1024)} %param.20) | copy-start | bytes 49156
  244.6 2.7 copy-start.2
  244.6 2.7 copy-start.9
  244.6 2.8 copy-start.11
  248.9 0.9 copy-start.7
  260.9 121.3 %all-to-all-start.2 = ((bf16[16,36,4096]{2,1,0:T(8,128)(2,1)}), bf16[16,36,4096]{2,1,0:T(8,128)(2,1)}, u32[]{:S(2)}, u32[]{:S(2)}) async-start(bf16[16,36,4096]{2,1,0:T(8,128)(2,1)} %bitcast.187), calls=%async_computation.4 | async-start | bytes 10485760 | tf_op jit(solution)/shard_map/all_to_all | solution.py:112
  386.9 120.0 %all-to-all-start = ((bf16[16,36,4096]{2,1,0:T(8,128)(2,1)}), bf16[16,36,4096]{2,1,0:T(8,128)(2,1)}, u32[]{:S(2)}, u32[]{:S(2)}) async-start(bf16[16,36,4096]{2,1,0:T(8,128)(2,1)} %bitcast.188), calls=%async_computation.1 | async-start | bytes 10485760 | tf_op jit(solution)/shard_map/all_to_all | solution.py:112
  506.9 119.8 %all-to-all-start.3 = ((bf16[16,36,4096]{2,1,0:T(8,128)(2,1)}), bf16[16,36,4096]{2,1,0:T(8,128)(2,1)}, u32[]{:S(2)}, u32[]{:S(2)}) async-start(bf16[16,36,4096]{2,1,0:T(8,128)(2,1)} %reshape.244), calls=%async_computation.5 | async-start | bytes 10485760 | tf_op jit(solution)/shard_map/all_to_all | solution.py:110
  543.8 88.4 %copy-start.8 = (bf16[96,4096]{1,0:T(8,128)(2,1)S(1)}, bf16[96,4096]{1,0:T(8,128)(2,1)}, u32[]{:S(2)}) copy-start(bf16[96,4096]{1,0:T(8,128)(2,1)} %copy-done.7) | copy-start | bytes 2359300
  543.8 88.4 %copy-start.13 = (bf16[4096,8]{0,1:T(8,128)(2,1)S(1)}, bf16[4096,8]{0,1:T(8,128)(2,1)}, u32[]{:S(2)}) copy-start(bf16[4096,8]{0,1:T(8,128)(2,1)} %param.21) | copy-start | bytes 196612
  543.8 88.9 %copy-start.6 = (bf16[96,4096]{1,0:T(8,128)(2,1)S(1)}, bf16[96,4096]{1,0:T(8,128)(2,1)}, u32[]{:S(2)}) copy-start(bf16[96,4096]{1,0:T(8,128)(2,1)} %get-tuple-element.14) | copy-start | bytes 2359300
  626.7 120.1 %all-to-all-start.1 = ((bf16[16,36,4096]{2,1,0:T(8,128)(2,1)}), bf16[16,36,4096]{2,1,0:T(8,128)(2,1)}, u32[]{:S(2)}, u32[]{:S(2)}) async-start(bf16[16,36,4096]{2,1,0:T(8,128)(2,1)} %reshape.237), calls=%async_computation.2 | async-start | bytes 10485760 | tf_op jit(solution)/shard_map/all_to_all | solution.py:110
  761.7 5.6 copy-start.4
  767.3 4.8 copy-start.5
  772.1 5.0 copy-start.3
  772.1 5.0 copy-start.10
  772.1 5.0 copy-start.12
  777.1 2.1 copy-start.1
Sparse Core Ops, SparseCore 0:
  8.9 148.0 all-gather.5
  165.9 37.9 reduce-scatter.4
  206.6 37.9 reduce-scatter.2
where the time goes:
time: 794 us; the launch traced here: 786 us
  waiting for transfers between devices  535 us (67%)
  local copies, waits for them, and re-layouts  78.5 us (10%)
  matrix products  76.2 us (10%)
  other arithmetic  36.6 us (5%)
  blocking collectives  24.1 us (3%)
  starting transfers between devices  21.8 us (3%)
  between operations  14 us (2%)
    all_to_all x2, waiting for transfers between devices, local(): lax.all_to_all(outgoing, ('expert', 'tensor'), split_axis=0, concat_axis=...  189 us
    all_to_all x2, waiting for transfers between devices, local(): lax.all_to_all(expert_rows(lax.all_to_all(outgoing, ('expert', 'tensor'),...  180 us
    all_gather x1, waiting for transfers between devices, local(): proj_full = lax.all_gather(out_proj, 'expert', axis=1, tiled=True)  122 us
    reduce_scatter x2, waiting for transfers between devices, local(): lax.psum_scatter(project(jnp.int32(0), tok_rows * lax.axis_size('tensor')...  44 us
    dot_general x2, matrix products, expert_rows(): jnp.dot(hidden, down_w, preferred_element_type=jnp.float32)  21.3 us
    broadcast_in_dim x4, local copies, waits for them, and re-layouts, local(): jnp.broadcast_to(packed, (n_experts, 2, capacity, model_width))  17.6 us
    dot_general x2, matrix products, project(): return jnp.dot(attended, proj_full, preferred_element_type=jnp.float32)  17.5 us
  transfers between devices with their start and end apart: 7, of which 7 were waited for; matrix products, arithmetic and copies ran while one was open for 16% of the time, Pallas kernels for 0%

commit v1 on v0

v1 whole, which is shorter than its diff:
```python
import math

import jax
import jax.numpy as jnp
from jax import lax
from jax.sharding import Mesh, PartitionSpec as P

HEADS = 32
KV = 2
HD = 128
TOPK = 2
SWAP = ((0, 1), (1, 0))
CHIPS = ("expert", "x")
TENSOR = ("x", "core")


epsilon = 1e-06


def attend_rows(query_block, key_all, value_all, segment_ids, kv_head):
    seq_rows = key_all.shape[0]
    heads_here = query_block.shape[-1] // HD
    key_head = lax.dynamic_slice_in_dim(key_all, kv_head * HD, HD, 1)
    value_head = lax.dynamic_slice_in_dim(value_all, kv_head * HD, HD, 1)
    query_heads = query_block.reshape(seq_rows, heads_here, HD)
    scores = jnp.einsum(
        "qhd,kd->hqk", query_heads, key_head, preferred_element_type=jnp.float32
    ) * (1.0 / math.sqrt(HD))
    positions = lax.broadcasted_iota(jnp.int32, (seq_rows, seq_rows), 0)
    columns = lax.broadcasted_iota(jnp.int32, (seq_rows, seq_rows), 1)
    allowed = (segment_ids[:, None] == segment_ids[None, :]) & (columns <= positions)
    masked = jnp.where(allowed[None], scores, -1e30)
    largest = jnp.max(masked, axis=-1, keepdims=True)
    powered = jnp.where(allowed[None], jnp.exp(masked - largest), 0.0)
    probs = (powered / jnp.sum(powered, axis=-1, keepdims=True)).astype(jnp.bfloat16)
    attended = jnp.einsum("hqk,kd->qhd", probs, value_head, preferred_element_type=jnp.float32)
    return attended.astype(jnp.bfloat16).reshape(seq_rows, heads_here * HD)


def expert_rows(rows_in, gate_w, up_w, down_w):
    flat_rows = rows_in.reshape(-1, rows_in.shape[-1])
    gate_val = jnp.dot(flat_rows, gate_w, preferred_element_type=jnp.float32)
    up_val = jnp.dot(flat_rows, up_w, preferred_element_type=jnp.float32)
    hidden = (jax.nn.silu(gate_val) * up_val).astype(jnp.bfloat16)
    result = jnp.dot(hidden, down_w, preferred_element_type=jnp.float32).astype(jnp.bfloat16)
    return result.reshape(rows_in.shape)


def local(
    stream,
    queries,
    key_rows,
    value_rows,
    segments,
    out_proj,
    norm_gain,
    router,
    routes,
    gate_proj,
    up_proj,
    down_proj,
):
    f32 = jnp.float32
    bf16 = jnp.bfloat16
    tensor_index = lax.axis_index(TENSOR)
    group_index = lax.axis_index("group")
    core_index = lax.axis_index("core")
    x_index = lax.axis_index("x")
    n_groups = lax.axis_size("group")
    n_x = lax.axis_size("x")
    micros = stream.shape[0]
    heads_here = queries.shape[-1] // HD
    kv_head = tensor_index * heads_here // (HEADS // KV)
    tok_rows = stream.shape[2]
    model_width = stream.shape[3]
    n_experts = router.shape[1]
    capacity = max(2, 3 * tok_rows * TOPK // (2 * n_experts))
    gate_w = gate_proj[0]
    up_w = up_proj[0]
    down_w = down_proj[0]
    proj_rows, proj_cols = out_proj.shape
    piece_rows = proj_rows // n_groups
    piece = lax.dynamic_slice_in_dim(out_proj, group_index * piece_rows, piece_rows, 0)
    pieces = lax.all_gather(piece, ("group", "expert"), axis=0, tiled=False)
    pieces = pieces.reshape(n_groups, -1, piece_rows, proj_cols)
    kv_width = key_rows.shape[-1]
    kv_all = lax.all_gather(
        jnp.concatenate([key_rows[:, 0], value_rows[:, 0]], axis=-1), TENSOR, axis=1, tiled=True
    )

    def project(rows):
        split_rows = rows.reshape(rows.shape[0], n_groups, piece_rows)
        return jnp.einsum(
            "tgk,gekn->ten", split_rows, pieces, preferred_element_type=f32
        ).reshape(rows.shape[0], model_width).astype(bf16)

    results = []
    for micro in range(micros):
        attended = attend_rows(
            queries[micro, 0],
            kv_all[micro, :, :kv_width],
            kv_all[micro, :, kv_width:],
            segments[micro, 0],
            kv_head,
        )
        by_core = attended.reshape(n_x, 2, tok_rows, attended.shape[-1])
        theirs = lax.dynamic_index_in_dim(by_core, 1 - core_index, 1, keepdims=False)
        mine = lax.dynamic_index_in_dim(by_core, core_index, 1, keepdims=False)
        theirs = project(theirs.reshape(n_x * tok_rows, -1))
        arrived = lax.ppermute(theirs, "core", SWAP)
        mine = project(mine.reshape(n_x * tok_rows, -1))
        on_chip = (mine.astype(f32) + arrived.astype(f32)).astype(bf16)
        if n_x == 2:
            by_x = on_chip.reshape(n_x, tok_rows, model_width)
            away = lax.dynamic_index_in_dim(by_x, 1 - x_index, 0, keepdims=False)
            here = lax.dynamic_index_in_dim(by_x, x_index, 0, keepdims=False)
            attn_out = here.astype(f32) + lax.ppermute(away, "x", SWAP).astype(f32)
        else:
            attn_out = lax.psum_scatter(
                on_chip, "x", scatter_dimension=0, tiled=True
            ).astype(f32)
        residual = stream[micro, 0].astype(f32) + attn_out
        scale = lax.rsqrt(jnp.mean(residual * residual, axis=-1, keepdims=True) + epsilon)
        normed = (residual * scale * norm_gain).astype(bf16)
        logits = jnp.dot(normed, router, preferred_element_type=f32)
        chosen = routes[micro, 0]
        expert_iota = lax.broadcasted_iota(jnp.int32, (1, 1, n_experts), 2)
        picks = chosen[:, :, None] == expert_iota
        picked = jnp.sum(jnp.where(picks, logits[:, None, :], 0.0), axis=-1)
        mixing = 1.0 / jnp.sum(jnp.exp(picked[:, None, :] - picked[:, :, None]), axis=-1)
        named = jnp.sum(picks.astype(bf16), axis=1)
        before = (
            lax.broadcasted_iota(jnp.int32, (tok_rows, tok_rows), 1)
            < lax.broadcasted_iota(jnp.int32, (tok_rows, tok_rows), 0)
        ).astype(bf16)
        slots = jnp.dot(before, named, preferred_element_type=f32).astype(jnp.int32)
        slot_hot = (
            slots[:, :, None] == lax.broadcasted_iota(jnp.int32, (1, 1, capacity), 2)
        ) & (named[:, :, None] > 0)
        placing = slot_hot.astype(bf16)
        expert_mix = jnp.sum(jnp.where(picks, mixing[:, :, None], 0.0), axis=1)
        mix_hot = jnp.where(slot_hot, expert_mix[:, :, None], 0.0)
        mix_high = mix_hot.astype(bf16)
        mix_low = (mix_hot - mix_high.astype(f32)).astype(bf16)
        packed = jnp.einsum("tec,td->ecd", placing, normed, preferred_element_type=f32).astype(bf16)
        own_rows = lax.all_to_all(packed, CHIPS, split_axis=0, concat_axis=0, tiled=True)
        sibling_rows = lax.ppermute(own_rows, "core", SWAP)
        sibling_out = expert_rows(sibling_rows, gate_w, up_w, down_w)
        sibling_half = lax.ppermute(sibling_out, "core", SWAP)
        own_out = expert_rows(own_rows, gate_w, up_w, down_w)
        summed = (own_out.astype(f32) + sibling_half.astype(f32)).astype(bf16)
        returned = lax.all_to_all(summed, CHIPS, split_axis=0, concat_axis=0, tiled=True)
        mixed = (
            residual
            + jnp.einsum("tec,ecd->td", mix_high, returned, preferred_element_type=f32)
            + jnp.einsum("tec,ecd->td", mix_low, returned, preferred_element_type=f32)
        )
        results.append(mixed.astype(bf16))
    return jnp.stack(results)[:, None]


def solution(mesh):
    n_group, n_expert, n_tensor = (mesh.shape[axis] for axis in ("group", "expert", "tensor"))
    fine = Mesh(
        mesh.devices.reshape(n_group, n_expert, n_tensor // 2, 2), ("group", "expert", "x", "core")
    )
    requests = ("group", "expert")
    rows = P(None, requests, TENSOR, None)
    halves = P(("expert", "x", "core"), None, None)
    return jax.shard_map(
        local,
        mesh=fine,
        in_specs=(
            rows,
            P(None, requests, None, TENSOR),
            rows,
            rows,
            P(None, requests, None),
            P(TENSOR, "expert"),
            P(),
            P(),
            rows,
            halves,
            halves,
            halves,
        ),
        out_specs=rows,
        check_vma=False,
    )
```

time: 794 us -> 584 us (0.74)
  the two profiles are of different devices: /device:TPU:11 before, /device:TPU:0 now
where the time goes in v1:
time: 584 us; the launch traced here: 574 us
  waiting for transfers between devices  287 us (49%)
  matrix products  113 us (19%)
  local copies, waits for them, and re-layouts  108 us (18%)
  starting transfers between devices  21 us (4%)
  other arithmetic  19.9 us (3%)
  between operations  14 us (2%)
  blocking collectives  10 us (2%)
    all_to_all x2, waiting for transfers between devices, local(): lax.all_to_all(packed, CHIPS, split_axis=0, concat_axis=0, tiled=True)  110 us
    all_gather x1, waiting for transfers between devices, local(): pieces = lax.all_gather(piece, ('group', 'expert'), axis=0, tiled=False)  85.6 us
    all_to_all x2, waiting for transfers between devices, local(): lax.all_to_all(summed, CHIPS, split_axis=0, concat_axis=0, tiled=True)  66.3 us
    dot_general x4, matrix products, project(): jnp.einsum('tgk,gekn->ten', split_rows, pieces, preferred_element_type=f32)  28.6 us
    dot_general x4, matrix products, expert_rows(): jnp.dot(hidden, down_w, preferred_element_type=jnp.float32)  28.5 us
    ppermute x2, waiting for transfers between devices, local(): attn_out = here.astype(f32) + lax.ppermute(away, 'x', SWAP).astype(f32)  25.6 us
    reshape x4, local copies, waits for them, and re-layouts, expert_rows(): return result.reshape(rows_in.shape)  17.2 us
    reshape x4, local copies, waits for them, and re-layouts, expert_rows(): flat_rows = rows_in.reshape(-1, rows_in.shape[-1])  16.5 us
  transfers between devices with their start and end apart: 13, of which 7 were waited for; matrix products, arithmetic and copies ran while one was open for 34% of the time, Pallas kernels for 0%

profile of v1, /device:TPU:0, one launch (start us, length us, event | category | flops | bytes accessed | tf_op | source)
XLA Modules:
  0.0 574.1 jit_solution(13372216441391228839)
XLA Ops:
  6.5 2.4 constant_dynamic-slice_fusion.3
  9.0 2.7 fusion.188
  11.8 2.3 copy.99
  15.1 10.0 %all_gather.9 = bf16[2,384,512]{2,1,0:T(8,128)(2,1)S(1)} all-gather(bf16[2,96,512]{2,1,0:T(8,128)(2,1)S(1)} %pad_maximum_fusion), channel_id=1, replica_groups=mesh['group'=2,'expert'=4,'x'=2,'core'=2] {'x','core'}, dimensions={1}, use_global_device_ids=true | all-gather | bytes 983040 | tf_op jit(solution)/shard_map/all_gather | solution.py:87
  25.9 5.4 fusion.190
  31.3 3.9 fusion.52
  35.2 2.5 copy.75
  37.7 2.2 reshape_reshape.18
  39.8 2.0 constant_dynamic-slice_fusion.4
  41.8 2.0 reshape_reshape.20
  43.9 2.3 copy.100
  46.1 5.4 fusion.195
  51.6 85.6 %all-gather.3.cloned.1.call-done = bf16[4096,1024]{1,0:T(8,128)(2,1)} async-done(((bf16[512,1024]{1,0:T(8,128)(2,1)}), bf16[4096,1024]{1,0:T(8,128)(2,1)}) %all-gather.3.cloned.1.call-update) | async-done | bytes 8388624 | tf_op jit(solution)/shard_map/all_gather | solution.py:84
  137.2 11.4 %copy.76 = bf16[2,4,512,1024]{2,3,1,0:T(8,128)(2,1)} copy(bf16[2,4,512,1024]{3,2,1,0:T(8,128)(2,1)} %bitcast.261) | data formatting | bytes 16777216 | tf_op jit(solution)/shard_map/reshape | solution.py:85
  148.6 7.7 %fusion.6 = bf16[192,4096]{1,0:T(8,128)(2,1)} fusion(bf16[4096,2,512]{2,0,1:T(8,128)(2,1)} %bitcast.262, bf16[192,2,512]{2,1,0:T(2,128)(2,1)} %reshape_reshape.20), kind=kOutput, calls=%fused_computation.18 | convolution fusion | flops 1611399168 | bytes 10354688 | tf_op jit(solution)/shard_map/tgk,gekn->ten/dot_general | solution.py:93
  157.8 2.5 copy.87
  160.3 2.3 reshape_reshape.21
  162.6 2.1 constant_dynamic-slice_fusion.1
  164.7 2.0 reshape_reshape.23
  166.7 7.6 %fusion.9 = bf16[192,4096]{1,0:T(8,128)(2,1)} fusion(bf16[4096,2,512]{2,0,1:T(8,128)(2,1)} %bitcast.263, bf16[192,2,512]{2,1,0:T(2,128)(2,1)} %reshape_reshape.23), kind=kOutput, calls=%fused_computation.21 | convolution fusion | flops 1611399168 | bytes 10354688 | tf_op jit(solution)/shard_map/tgk,gekn->ten/dot_general | solution.py:93
  177.1 6.8 %add_convert_fusion.3 = bf16[192,4096]{1,0:T(8,128)(2,1)S(1)} fusion(bf16[192,4096]{1,0:T(8,128)(2,1)} %collective-permute-done, bf16[4096,2,512]{2,0,1:T(8,128)(2,1)} %bitcast.264, bf16[192,2,512]{2,1,0:T(2,128)(2,1)} %reshape_reshape.19), kind=kOutput, calls=%fused_computation.63 | convolution fusion | flops 1614544896 | bytes 11927552 | tf_op jit(solution)/shard_map/tgk,gekn->ten/dot_general | solution.py:93
  186.4 6.7 %add_convert_fusion.2 = bf16[192,4096]{1,0:T(8,128)(2,1)S(1)} fusion(bf16[192,4096]{1,0:T(8,128)(2,1)} %collective-permute-done.4, bf16[4096,2,512]{2,0,1:T(8,128)(2,1)} %bitcast.265, bf16[192,2,512]{2,1,0:T(2,128)(2,1)S(1)} %reshape_reshape.22), kind=kOutput, calls=%fused_computation.62 | convolution fusion | flops 1614544896 | bytes 11927552 | tf_op jit(solution)/shard_map/tgk,gekn->ten/dot_general | solution.py:93
  195.9 9.7 %collective-permute-done.1 = bf16[96,4096]{1,0:T(8,128)(2,1)} collective-permute-done((bf16[96,4096]{1,0:T(8,128)(2,1)}, bf16[96,4096]{1,0:T(8,128)(2,1)}, u32[]{:S(2)}, u32[]{:S(2)}) %collective-permute-start.1) | collective-permute-done | bytes 786464 | tf_op jit(solution)/shard_map/ppermute | solution.py:117
  205.7 15.9 %collective-permute-done.5 = bf16[96,4096]{1,0:T(8,128)(2,1)} collective-permute-done((bf16[96,4096]{1,0:T(8,128)(2,1)}, bf16[96,4096]{1,0:T(8,128)(2,1)}, u32[]{:S(2)}, u32[]{:S(2)}) %collective-permute-start.5) | collective-permute-done | bytes 786464 | tf_op jit(solution)/shard_map/ppermute | solution.py:117
  221.6 3.3 multiply_reduce_fusion.1
  224.9 3.2 multiply_convert_fusion.1
  229.0 2.4 convolution_convert_fusion
  231.3 4.4 all-to-all-start.2
  235.9 3.5 convolution_convert_fusion.1
  239.4 55.5 %all-to-all-done.2 = bf16[8,36,4096]{2,1,0:T(8,128)(2,1)} async-done(((bf16[8,36,4096]{2,1,0:T(8,128)(2,1)}), bf16[8,36,4096]{2,1,0:T(8,128)(2,1)}, u32[]{:S(2)}, u32[]{:S(2)}) %all-to-all-start.2) | async-done | bytes 2359328 | tf_op jit(solution)/shard_map/all_to_all | solution.py:146
  294.8 4.8 all-to-all-start
  299.6 4.5 copy.90
  304.1 54.5 %all-to-all-done = bf16[8,36,4096]{2,1,0:T(8,128)(2,1)} async-done(((bf16[8,36,4096]{2,1,0:T(8,128)(2,1)}), bf16[8,36,4096]{2,1,0:T(8,128)(2,1)}, u32[]{:S(2)}, u32[]{:S(2)}) %all-to-all-start) | async-done | bytes 2359328 | tf_op jit(solution)/shard_map/all_to_all | solution.py:146
  358.6 4.5 copy.79
  363.1 4.5 copy.91
  367.6 4.1 reshape.190
  371.7 4.8 fusion.24
  376.5 6.8 %convolution_convert_fusion.2 = bf16[288,4096]{1,0:T(8,128)(2,1)} fusion(bf16[1,384,4096]{2,1,0:T(8,128)(2,1)S(1)} %copy-done, f32[288,384]{1,0:T(8,128)} %fusion.24, bf16[288,4096]{1,0:T(8,128)(2,1)} %reshape.190, bf16[1,4096,384]{2,1,0:T(8,128)(2,1)} %param.21), kind=kOutput, calls=%fused_computation.4 | convolution fusion | flops 1813782528 | bytes 11452416 | tf_op jit(solution)/shard_map/dot_general | solution.py:45
  383.3 4.1 reshape.191
  387.4 4.5 copy.92
  392.4 4.1 reshape.189
  396.5 4.8 fusion.34
  401.2 7.5 %fusion.2 = f32[288,4096]{1,0:T(8,128)} fusion(bf16[1,384,4096]{2,1,0:T(8,128)(2,1)S(1)} %copy-done, bf16[288,4096]{1,0:T(8,128)(2,1)} %reshape.189, bf16[1,4096,384]{2,1,0:T(8,128)(2,1)} %param.22, f32[288,384]{1,0:T(8,128)} %fusion.34), kind=kOutput, calls=%fused_computation.6 | convolution fusion | flops 1814962176 | bytes 13811712 | tf_op jit(solution)/shard_map/dot_general | solution.py:45
  408.7 5.3 reshape.197
  414.1 4.4 copy.80
  418.5 4.1 reshape.186
  422.7 4.9 fusion.28
  427.6 4.8 add_convert_fusion
  432.4 4.4 all-to-all-start.3
  436.8 6.7 %convolution_convert_fusion.4 = bf16[288,4096]{1,0:T(8,128)(2,1)} fusion(bf16[1,384,4096]{2,1,0:T(8,128)(2,1)S(1)} %copy-done, f32[288,384]{1,0:T(8,128)} %fusion.28, bf16[288,4096]{1,0:T(8,128)(2,1)} %reshape.186, bf16[1,4096,384]{2,1,0:T(8,128)(2,1)} %param.21), kind=kOutput, calls=%fused_computation.7 | convolution fusion | flops 1813782528 | bytes 11452416 | tf_op jit(solution)/shard_map/dot_general | solution.py:45
  443.5 4.1 reshape.187
  447.7 4.5 copy.81
  452.2 4.1 reshape.185
  456.3 4.8 fusion.38
  461.0 7.5 %fusion.3 = f32[288,4096]{1,0:T(8,128)} fusion(bf16[1,384,4096]{2,1,0:T(8,128)(2,1)S(1)} %copy-done, bf16[288,4096]{1,0:T(8,128)(2,1)} %reshape.185, bf16[1,4096,384]{2,1,0:T(8,128)(2,1)} %param.22, f32[288,384]{1,0:T(8,128)} %fusion.38), kind=kOutput, calls=%fused_computation.9 | convolution fusion | flops 1814962176 | bytes 13811712 | tf_op jit(solution)/shard_map/dot_general | solution.py:45
  468.5 5.2 reshape.194
  473.8 6.3 %add_convert_fusion.1 = bf16[8,36,4096]{2,1,0:T(8,128)(2,1)} fusion(f32[8,36,4096]{2,1,0:T(8,128)} %reshape.194, bf16[8,36,4096]{2,0,1:T(8,128)(2,1)} %collective-permute-done.3), kind=kLoop, calls=%fused_computation.11 | loop fusion | flops 3538944 | bytes 9437184 | tf_op jit(solution)/shard_map/convert_element_type | solution.py:151
  480.1 16.6 %all-to-all-done.3 = bf16[8,36,4096]{2,1,0:T(8,128)(2,1)} async-done(((bf16[8,36,4096]{2,1,0:T(8,128)(2,1)}), bf16[8,36,4096]{2,1,0:T(8,128)(2,1)}, u32[]{:S(2)}, u32[]{:S(2)}) %all-to-all-start.3) | async-done | bytes 2359328 | tf_op jit(solution)/shard_map/all_to_all | solution.py:152
  496.7 4.4 all-to-all-start.1
  504.3 2.5 convolution_bitcast_fusion.4
  506.8 3.7 fusion.17
  510.5 49.7 %all-to-all-done.1 = bf16[8,36,4096]{2,1,0:T(8,128)(2,1)} async-done(((bf16[8,36,4096]{2,1,0:T(8,128)(2,1)}), bf16[8,36,4096]{2,1,0:T(8,128)(2,1)}, u32[]{:S(2)}, u32[]{:S(2)}) %all-to-all-start.1) | async-done | bytes 2359328 | tf_op jit(solution)/shard_map/all_to_all | solution.py:152
  560.2 2.6 convolution_bitcast_fusion.6
  562.8 2.9 fusion.16
  (87 shorter events, 17.7 us)
Async XLA Ops:
  6.5 369.9 %copy-start = (bf16[1,384,4096]{2,1,0:T(8,128)(2,1)S(1)}, bf16[1,384,4096]{2,1,0:T(8,128)(2,1)}, u32[]{:S(2)}) copy-start(bf16[1,384,4096]{2,1,0:T(8,128)(2,1)} %param.23) | copy-start | bytes 9437188
  6.5 130.6 %all-gather.3.cloned.1.call-start = ((), (), s32[]{:S(2)}) async-start(), calls=%async_computation.4 | async-start | bytes 9437184 | tf_op jit(solution)/shard_map/all_gather | solution.py:84
  9.0 5.1 copy-start.18
  9.0 5.1 copy-start.15
  9.0 5.1 copy-start.16
  148.6 7.7 %copy-start.14 = (bf16[1,384,256]{2,1,0:T(8,128)(2,1)S(1)}, bf16[1,384,256]{2,1,0:T(8,128)(2,1)}, u32[]{:S(2)}) copy-start(bf16[1,384,256]{2,1,0:T(8,128)(2,1)} %get-tuple-element.15) | copy-start | bytes 589828
  148.6 7.7 %copy-start.20 = (f32[8,384,384]{1,2,0:T(8,128)S(1)}, f32[8,384,384]{1,2,0:T(8,128)}, u32[]{:S(2)}) copy-start(f32[8,384,384]{1,2,0:T(8,128)} %get-tuple-element.26) | copy-start | bytes 14155780
  156.3 20.8 %collective-permute-start = (bf16[192,4096]{1,0:T(8,128)(2,1)}, bf16[192,4096]{1,0:T(8,128)(2,1)}, u32[]{:S(2)}, u32[]{:S(2)}) collective-permute-start(bf16[192,4096]{1,0:T(8,128)(2,1)} %fusion.6), channel_id=1, source_target_pairs={{0,1},{1,0},{2,3},{3,2},{4,5},{5,4},{6,7},{7,6},{8,9},{9,8},{10,11... | collective-permute-start | bytes 4718600 | tf_op jit(solution)/shard_map/ppermute | solution.py:110
  174.2 12.2 %collective-permute-start.4 = (bf16[192,4096]{1,0:T(8,128)(2,1)}, bf16[192,4096]{1,0:T(8,128)(2,1)}, u32[]{:S(2)}, u32[]{:S(2)}) collective-permute-start(bf16[192,4096]{1,0:T(8,128)(2,1)} %fusion.9), channel_id=1, source_target_pairs={{0,1},{1,0},{2,3},{3,2},{4,5},{5,4},{6,7},{7,6},{8,9},{9,8},{10,11... | collective-permute-start | bytes 4718600 | tf_op jit(solution)/shard_map/ppermute | solution.py:110
  183.9 9.2 %copy-start.6 = (bf16[192,4096]{1,0:T(8,128)(2,1)}, bf16[192,4096]{1,0:T(8,128)(2,1)S(1)}, u32[]{:S(2)}) copy-start(bf16[192,4096]{1,0:T(8,128)(2,1)S(1)} %add_convert_fusion.3) | copy-start | bytes 4718596
  184.9 10.8 %copy-start.19 = (s32[2,1,96,2]{2,3,1,0:T(2,128)S(1)}, s32[2,1,96,2]{2,3,1,0:T(2,128)}, u32[]{:S(2)}) copy-start(s32[2,1,96,2]{2,3,1,0:T(2,128)} %param.20) | copy-start | bytes 4612
  184.9 20.7 %collective-permute-start.1 = (bf16[96,4096]{1,0:T(8,128)(2,1)}, bf16[96,4096]{1,0:T(8,128)(2,1)}, u32[]{:S(2)}, u32[]{:S(2)}) collective-permute-start(bf16[96,4096]{1,0:T(8,128)(2,1)} %dynamic-slice_bitcast_fusion.1), channel_id=1, source_target_pairs={{0,2},{2,0},{1,3},{3,1},{4,6},{6,4},{5,7},{7,5},{8,10},{10,8},{9,1... | collective-permute-start | bytes 2359304 | tf_op jit(solution)/shard_map/ppermute | solution.py:117
  193.1 1.2 copy-start.9
  195.2 29.6 %copy-start.17 = (f32[4096]{0:T(1024)S(1)}, f32[4096]{0:T(1024)}, u32[]{:S(2)}) copy-start(f32[4096]{0:T(1024)} %param.18) | copy-start | bytes 49156
  195.2 26.4 %collective-permute-start.5 = (bf16[96,4096]{1,0:T(8,128)(2,1)}, bf16[96,4096]{1,0:T(8,128)(2,1)}, u32[]{:S(2)}, u32[]{:S(2)}) collective-permute-start(bf16[96,4096]{1,0:T(8,128)(2,1)} %dynamic-slice_bitcast_fusion), channel_id=1, source_target_pairs={{0,2},{2,0},{1,3},{3,1},{4,6},{6,4},{5,7},{7,5},{8,10},{10,8},{9,1... | collective-permute-start | bytes 2359304 | tf_op jit(solution)/shard_map/ppermute | solution.py:117
  195.8 29.1 %copy-start.2 = (bf16[2,1,96,4096]{3,2,1,0:T(8,128)(2,1)S(1)}, bf16[2,1,96,4096]{3,2,1,0:T(8,128)(2,1)}, u32[]{:S(2)}) copy-start(bf16[2,1,96,4096]{3,2,1,0:T(8,128)(2,1)} %param.12) | copy-start | bytes 4718596
  195.8 29.1 %copy-start.7 = (bf16[192,4096]{1,0:T(8,128)(2,1)S(1)}, bf16[192,4096]{1,0:T(8,128)(2,1)}, u32[]{:S(2)}) copy-start(bf16[192,4096]{1,0:T(8,128)(2,1)} %copy-done.6) | copy-start | bytes 4718596
  195.8 29.1 %copy-start.10 = (bf16[192,4096]{1,0:T(8,128)(2,1)S(1)}, bf16[192,4096]{1,0:T(8,128)(2,1)}, u32[]{:S(2)}) copy-start(bf16[192,4096]{1,0:T(8,128)(2,1)} %copy-done.9) | copy-start | bytes 4718596
  228.1 0.9 copy-start.5
  231.3 63.5 %all-to-all-start.2 = ((bf16[8,36,4096]{2,1,0:T(8,128)(2,1)}), bf16[8,36,4096]{2,1,0:T(8,128)(2,1)}, u32[]{:S(2)}, u32[]{:S(2)}) async-start(bf16[8,36,4096]{2,1,0:T(8,128)(2,1)} %convolution_convert_fusion), calls=%async_computation.2 | async-start | bytes 5242880 | tf_op jit(solution)/shard_map/all_to_all | solution.py:146
  294.8 63.8 %all-to-all-start = ((bf16[8,36,4096]{2,1,0:T(8,128)(2,1)}), bf16[8,36,4096]{2,1,0:T(8,128)(2,1)}, u32[]{:S(2)}, u32[]{:S(2)}) async-start(bf16[8,36,4096]{2,1,0:T(8,128)(2,1)} %convolution_convert_fusion.1), calls=%async_computation | async-start | bytes 5242880 | tf_op jit(solution)/shard_map/all_to_all | solution.py:146
  304.1 59.0 %collective-permute-start.6 = (bf16[8,36,4096]{2,0,1:T(8,128)(2,1)}, bf16[8,36,4096]{2,0,1:T(8,128)(2,1)}, u32[]{:S(2)}, u32[]{:S(2)}) collective-permute-start(bf16[8,36,4096]{2,0,1:T(8,128)(2,1)} %copy.90), channel_id=1, source_target_pairs={{0,1},{1,0},{2,3},{3,2},{4,5},{5,4},{6,7},{7,6},{8,9},{9,8},{10,11... | collective-permute-start | bytes 7077896 | tf_op jit(solution)/shard_map/ppermute | solution.py:147
  363.1 51.0 %collective-permute-start.2 = (bf16[8,36,4096]{2,0,1:T(8,128)(2,1)}, bf16[8,36,4096]{2,0,1:T(8,128)(2,1)}, u32[]{:S(2)}, u32[]{:S(2)}) collective-permute-start(bf16[8,36,4096]{2,0,1:T(8,128)(2,1)} %copy.79), channel_id=1, source_target_pairs={{0,1},{1,0},{2,3},{3,2},{4,5},{5,4},{6,7},{7,6},{8,9},{9,8},{10,11... | collective-permute-start | bytes 7077896 | tf_op jit(solution)/shard_map/ppermute | solution.py:147
  391.9 35.7 %collective-permute-start.7 = (bf16[8,36,4096]{2,0,1:T(8,128)(2,1)}, bf16[8,36,4096]{2,0,1:T(8,128)(2,1)}, u32[]{:S(2)}, u32[]{:S(2)}) collective-permute-start(bf16[8,36,4096]{2,0,1:T(8,128)(2,1)} %copy.92), channel_id=1, source_target_pairs={{0,1},{1,0},{2,3},{3,2},{4,5},{5,4},{6,7},{7,6},{8,9},{9,8},{10,11... | collective-permute-start | bytes 7077896 | tf_op jit(solution)/shard_map/ppermute | solution.py:149
  422.7 4.9 copy-start.1
  432.4 64.3 %all-to-all-start.3 = ((bf16[8,36,4096]{2,1,0:T(8,128)(2,1)}), bf16[8,36,4096]{2,1,0:T(8,128)(2,1)}, u32[]{:S(2)}, u32[]{:S(2)}) async-start(bf16[8,36,4096]{2,1,0:T(8,128)(2,1)} %add_convert_fusion), calls=%async_computation.3 | async-start | bytes 5242880 | tf_op jit(solution)/shard_map/all_to_all | solution.py:152
  452.2 21.6 %collective-permute-start.3 = (bf16[8,36,4096]{2,0,1:T(8,128)(2,1)}, bf16[8,36,4096]{2,0,1:T(8,128)(2,1)}, u32[]{:S(2)}, u32[]{:S(2)}) collective-permute-start(bf16[8,36,4096]{2,0,1:T(8,128)(2,1)} %copy.81), channel_id=1, source_target_pairs={{0,1},{1,0},{2,3},{3,2},{4,5},{5,4},{6,7},{7,6},{8,9},{9,8},{10,11... | collective-permute-start | bytes 7077896 | tf_op jit(solution)/shard_map/ppermute | solution.py:149
  480.1 21.0 %copy-start.13 = (bf16[4096,8]{0,1:T(8,128)(2,1)S(1)}, bf16[4096,8]{0,1:T(8,128)(2,1)}, u32[]{:S(2)}) copy-start(bf16[4096,8]{0,1:T(8,128)(2,1)} %param.19) | copy-start | bytes 196612
  496.7 63.5 %all-to-all-start.1 = ((bf16[8,36,4096]{2,1,0:T(8,128)(2,1)}), bf16[8,36,4096]{2,1,0:T(8,128)(2,1)}, u32[]{:S(2)}, u32[]{:S(2)}) async-start(bf16[8,36,4096]{2,1,0:T(8,128)(2,1)} %add_convert_fusion.1), calls=%async_computation.1 | async-start | bytes 5242880 | tf_op jit(solution)/shard_map/all_to_all | solution.py:152
  502.5 4.2 copy-start.3
  502.5 4.2 copy-start.11
  560.2 2.6 copy-start.4
  560.2 2.7 copy-start.8
  562.8 2.9 copy-start.12
Sparse Core Ops, SparseCore 0:
  9.5 127.6 all-gather.2

commit v2 on v1

--- a/solution.py
+++ b/solution.py
@@ -1,8 +1,11 @@
+import functools
 import math
 
 import jax
 import jax.numpy as jnp
 from jax import lax
+from jax.experimental import pallas as pl
+from jax.experimental.pallas import tpu as pltpu
 from jax.sharding import Mesh, PartitionSpec as P
 
 HEADS = 32
@@ -37,13 +40,124 @@
     return attended.astype(jnp.bfloat16).reshape(seq_rows, heads_here * HD)
 
 
-def expert_rows(rows_in, gate_w, up_w, down_w):
-    flat_rows = rows_in.reshape(-1, rows_in.shape[-1])
-    gate_val = jnp.dot(flat_rows, gate_w, preferred_element_type=jnp.float32)
-    up_val = jnp.dot(flat_rows, up_w, preferred_element_type=jnp.float32)
-    hidden = (jax.nn.silu(gate_val) * up_val).astype(jnp.bfloat16)
-    result = jnp.dot(hidden, down_w, preferred_element_type=jnp.float32).astype(jnp.bfloat16)
-    return result.reshape(rows_in.shape)
+def experts_kernel(
+    n_chunks,
+    rows_ref,
+    gate_ref,
+    up_ref,
+    down_ref,
+    out_ref,
+    mine,
+    theirs,
+    part_out,
+    part_in,
+    row_send,
+    row_recv,
+    part_send,
+    part_recv,
+):
+    sibling = {"core": 1 - lax.axis_index("core")}
+    n_blocks, block_rows, width = rows_ref.shape
+    stride = mine.shape[0] // n_blocks
+    chunk_blocks = n_blocks // n_chunks
+    chunk_rows = chunk_blocks * stride
+    whole_rows = block_rows // 16 * 16
+    barrier = pltpu.get_barrier_semaphore()
+    pl.semaphore_signal(barrier, inc=1, device_id=sibling, device_id_type=pl.DeviceIdType.MESH)
+
+    def stage(chunk):
+        for block in range(chunk * chunk_blocks, (chunk + 1) * chunk_blocks):
+            base = block * stride
+            if whole_rows:
+                mine[base : base + whole_rows] = rows_ref[block, :whole_rows]
+            if whole_rows < block_rows:
+                rest = rows_ref[block, whole_rows:].astype(jnp.float32)
+                filler = jnp.zeros((16 - block_rows + whole_rows, width), jnp.float32)
+                mine[base + whole_rows : base + stride] = jnp.concatenate(
+                    [rest, filler], axis=0
+                ).astype(jnp.bfloat16)
+
+    def send(source, target, send_sem, recv_sem, chunk):
+        part = pl.ds(chunk * chunk_rows, chunk_rows)
+        return pltpu.make_async_remote_copy(
+            src_ref=source.at[part],
+            dst_ref=target.at[part],
+            send_sem=send_sem.at[chunk],
+            recv_sem=recv_sem.at[chunk],
+            device_id=sibling,
+            device_id_type=pl.DeviceIdType.MESH,
+        )
+
+    def hidden_of(source, chunk):
+        rows = source[chunk * chunk_rows : (chunk + 1) * chunk_rows]
+        gate_val = jnp.dot(rows, gate_ref[...], preferred_element_type=jnp.float32)
+        up_val = jnp.dot(rows, up_ref[...], preferred_element_type=jnp.float32)
+        return (gate_val / (1.0 + jnp.exp(-gate_val)) * up_val).astype(jnp.bfloat16)
+
+    tile = min(width, 1024)
+    row_copies = [send(mine, theirs, row_send, row_recv, chunk) for chunk in range(n_chunks)]
+    part_copies = [send(part_out, part_in, part_send, part_recv, c) for c in range(n_chunks)]
+    for chunk in range(n_chunks):
+        stage(chunk)
+        if chunk == 0:
+            pl.semaphore_wait(barrier, 1)
+        row_copies[chunk].start()
+    for chunk in range(n_chunks):
+        row_copies[chunk].wait_recv()
+        hidden = hidden_of(theirs, chunk)
+        for column in range(0, width, tile):
+            part_out[chunk * chunk_rows : (chunk + 1) * chunk_rows, column : column + tile] = (
+                jnp.dot(
+                    hidden,
+                    down_ref[:, column : column + tile],
+                    preferred_element_type=jnp.float32,
+                ).astype(jnp.bfloat16)
+            )
+        part_copies[chunk].start()
+    for chunk in range(n_chunks):
+        hidden = hidden_of(mine, chunk)
+        part_copies[chunk].wait_recv()
+        for column in range(0, width, tile):
+            here = jnp.dot(
+                hidden, down_ref[:, column : column + tile], preferred_element_type=jnp.float32
+            ).astype(jnp.bfloat16)
+            other = part_in[chunk * chunk_rows : (chunk + 1) * chunk_rows, column : column + tile]
+            both = (here.astype(jnp.float32) + other.astype(jnp.float32)).astype(jnp.bfloat16)
+            for block in range(chunk_blocks):
+                out_ref[chunk * chunk_blocks + block, :, column : column + tile] = both[
+                    block * stride : block * stride + block_rows
+                ]
+    for chunk in range(n_chunks):
+        row_copies[chunk].wait_send()
+        part_copies[chunk].wait_send()
+
+
+def run_experts(rows_in, gate_w, up_w, down_w):
+    given = rows_in.shape
+    width = given[-1]
+    if given[1] < 16:
+        rows_in = rows_in.reshape(-1, given[1] * (16 // given[1]), width)
+    n_blocks, block_rows, _ = rows_in.shape
+    stride = -(-block_rows // 16) * 16
+    n_chunks = 2
+    buffer = pltpu.VMEM((n_blocks * stride, width), jnp.bfloat16)
+    sems = pltpu.SemaphoreType.DMA((n_chunks,))
+    result = pl.pallas_call(
+        functools.partial(experts_kernel, n_chunks),
+        out_shape=jax.ShapeDtypeStruct(rows_in.shape, jnp.bfloat16),
+        in_specs=[pl.BlockSpec(memory_space=pltpu.VMEM)] * 4,
+        out_specs=pl.BlockSpec(memory_space=pltpu.VMEM),
+        scratch_shapes=[buffer] * 4 + [sems] * 4,
+        compiler_params=pltpu.CompilerParams(
+            collective_id=0, has_side_effects=True, vmem_limit_bytes=44 * 1024 * 1024
+        ),
+        cost_estimate=pl.CostEstimate(
+            flops=12 * n_blocks * block_rows * width * gate_w.shape[1],
+            bytes_accessed=2 * (3 * width * gate_w.shape[1] + 6 * n_blocks * block_rows * width),
+            transcendentals=0,
+        ),
+    )(rows_in, gate_w, up_w, down_w)
+    return result.reshape(given)
 
 
 def local(
@@ -144,11 +258,7 @@
         mix_low = (mix_hot - mix_high.astype(f32)).astype(bf16)
         packed = jnp.einsum("tec,td->ecd", placing, normed, preferred_element_type=f32).astype(bf16)
         own_rows = lax.all_to_all(packed, CHIPS, split_axis=0, concat_axis=0, tiled=True)
-        sibling_rows = lax.ppermute(own_rows, "core", SWAP)
-        sibling_out = expert_rows(sibling_rows, gate_w, up_w, down_w)
-        sibling_half = lax.ppermute(sibling_out, "core", SWAP)
-        own_out = expert_rows(own_rows, gate_w, up_w, down_w)
-        summed = (own_out.astype(f32) + sibling_half.astype(f32)).astype(bf16)
+        summed = run_experts(own_rows, gate_w, up_w, down_w)
         returned = lax.all_to_all(summed, CHIPS, split_axis=0, concat_axis=0, tiled=True)
         mixed = (
             residual

time: 584 us -> 493 us (0.84)
  local copies, waits for them, and re-layouts: 108 us -> 27.8 us
  matrix products: 113 us -> 57.4 us
  Pallas kernels: 0 us -> 36.7 us
  waiting for transfers between devices: 287 us -> 314 us
  other arithmetic: 19.9 us -> 6.03 us
    dot_general x8 -> x0, matrix products: 47.7 us -> none  [the longest x4 28.5 us: expert_rows(): jnp.dot(hidden, down_w, preferred_element_type=jnp.float32)]
    pallas_call x0 -> x2, Pallas kernels: none -> 36.7 us  [run_experts(): pl.pallas_call(functools.partial(experts_kernel, n_chunks), out_shape=jax...]
    reshape x8 -> x0, local copies, waits for them, and re-layouts: 33.7 us -> none  [the longest x4 17.2 us: expert_rows(): return result.reshape(rows_in.shape)]
    all_to_all x2, waiting for transfers between devices: 66.3 us -> 91.1 us  [local(): lax.all_to_all(summed, CHIPS, split_axis=0, concat_axis=0, tiled=True)]
    all_gather x1, waiting for transfers between devices: 85.6 us -> 102 us  [local(): pieces = lax.all_gather(piece, ('group', 'expert'), axis=0, tiled=False)]
    all_to_all x2, waiting for transfers between devices: 110 us -> 94.7 us  [local(): lax.all_to_all(packed, CHIPS, split_axis=0, concat_axis=0, tiled=True)]
    convert_element_type x2 -> x0, other arithmetic: 11 us -> none  [local(): summed = (own_out.astype(f32) + sibling_half.astype(f32)).astype(bf16)]
    convert_element_type x2 -> x0, local copies, waits for them, and re-layouts: 10.6 us -> none  [local(): summed = (own_out.astype(f32) + sibling_half.astype(f32)).astype(bf16)]
  transfers between devices with their start and end apart: 13 -> 9, of which waited for: 7 -> 7; matrix products, arithmetic and copies ran while one was open for 34% -> 10% of each run, Pallas kernels for 0% -> 8%
where the time goes in v2:
time: 493 us; the launch traced here: 486 us
  waiting for transfers between devices  314 us (64%)
  matrix products  57.4 us (12%)
  Pallas kernels  36.7 us (7%)
  local copies, waits for them, and re-layouts  27.8 us (6%)
  starting transfers between devices  20.2 us (4%)
  between operations  14.1 us (3%)
  blocking collectives  10 us (2%)
  other arithmetic  6.03 us (1%)
    all_gather x1, waiting for transfers between devices, local(): pieces = lax.all_gather(piece, ('group', 'expert'), axis=0, tiled=False)  102 us
    all_to_all x2, waiting for transfers between devices, local(): lax.all_to_all(packed, CHIPS, split_axis=0, concat_axis=0, tiled=True)  94.7 us
    all_to_all x2, waiting for transfers between devices, local(): lax.all_to_all(summed, CHIPS, split_axis=0, concat_axis=0, tiled=True)  91.1 us
    pallas_call x2, Pallas kernels, run_experts(): pl.pallas_call(functools.partial(experts_kernel, n_chunks), out_shape=jax...  36.7 us
    dot_general x4, matrix products, project(): jnp.einsum('tgk,gekn->ten', split_rows, pieces, preferred_element_type=f32)  28.3 us
    ppermute x2, waiting for transfers between devices, local(): attn_out = here.astype(f32) + lax.ppermute(away, 'x', SWAP).astype(f32)  25.5 us
    reshape x1, local copies, waits for them, and re-layouts, local(): pieces = pieces.reshape(n_groups, -1, piece_rows, proj_cols)  11.6 us
    all_gather x1, blocking collectives, local(): lax.all_gather(jnp.concatenate([key_rows[:, 0], value_rows[:, 0]], axis=-...  10 us
  transfers between devices with their start and end apart: 9, of which 7 were waited for; matrix products, arithmetic and copies ran while one was open for 10% of the time, Pallas kernels for 8%

profile of v2, /device:TPU:0, one launch (start us, length us, event | category | flops | bytes accessed | tf_op | source)
XLA Modules:
  0.0 486.2 jit_solution(10870775012959622036)
XLA Ops:
  6.5 1.6 copy-done
  8.1 1.0 constant_dynamic-slice_fusion.3
  9.2 1.5 fusion.124
  10.7 0.4 copy.63
  11.1 0.3 copy-done.27
  11.4 0.2 copy-done.24
  11.7 0.2 fusion.34
  11.9 10.0 %all_gather.9 = bf16[2,384,512]{2,1,0:T(8,128)(2,1)S(1)} all-gather(bf16[2,96,512]{2,1,0:T(8,128)(2,1)S(1)} %pad_maximum_fusion), channel_id=1, replica_groups=mesh['group'=2,'expert'=4,'x'=2,'core'=2] {'x','core'}, dimensions={1}, use_global_device_ids=true | all-gather | bytes 983040 | tf_op jit(solution)/shard_map/all_gather | solution.py:201
  22.0 4.1 fusion.126
  26.1 3.0 fusion.30
  29.1 0.5 copy.47
  29.6 0.3 reshape_reshape.18
  29.9 0.1 constant_dynamic-slice_fusion.4
  30.0 0.3 reshape_reshape.20
  30.3 0.4 copy.64
  30.6 4.1 fusion.131
  34.7 102.4 %all-gather.3.cloned.1.call-done = bf16[4096,1024]{1,0:T(8,128)(2,1)} async-done(((bf16[512,1024]{1,0:T(8,128)(2,1)}), bf16[4096,1024]{1,0:T(8,128)(2,1)}) %all-gather.3.cloned.1.call-update) | async-done | bytes 8388624 | tf_op jit(solution)/shard_map/all_gather | solution.py:198
  137.2 11.6 %copy.48 = bf16[2,4,512,1024]{2,3,1,0:T(8,128)(2,1)} copy(bf16[2,4,512,1024]{3,2,1,0:T(8,128)(2,1)} %bitcast.211) | data formatting | bytes 16777216 | tf_op jit(solution)/shard_map/reshape | solution.py:199
  148.8 7.5 %fusion.4 = bf16[192,4096]{1,0:T(8,128)(2,1)} fusion(bf16[4096,2,512]{2,0,1:T(8,128)(2,1)} %bitcast.212, bf16[192,2,512]{2,1,0:T(2,128)(2,1)S(1)} %reshape_reshape.20), kind=kOutput, calls=%fused_computation.10 | convolution fusion | flops 1611399168 | bytes 10354688 | tf_op jit(solution)/shard_map/tgk,gekn->ten/dot_general | solution.py:207
  156.3 0.6 fusion.31
  156.9 0.5 copy.55
  157.5 0.3 reshape_reshape.21
  157.8 0.1 constant_dynamic-slice_fusion.1
  157.9 0.3 reshape_reshape.23
  158.2 7.5 %fusion.7 = bf16[192,4096]{1,0:T(8,128)(2,1)} fusion(bf16[4096,2,512]{2,0,1:T(8,128)(2,1)} %bitcast.213, bf16[192,2,512]{2,1,0:T(2,128)(2,1)S(1)} %reshape_reshape.23), kind=kOutput, calls=%fused_computation.13 | convolution fusion | flops 1611399168 | bytes 10354688 | tf_op jit(solution)/shard_map/tgk,gekn->ten/dot_general | solution.py:207
  165.6 0.5 collective-permute-start.2
  166.1 0.3 reshape_reshape.19
  166.4 0.3 reshape_reshape.22
  166.7 6.7 %add_convert_fusion.1 = bf16[192,4096]{1,0:T(8,128)(2,1)S(1)} fusion(bf16[192,4096]{1,0:T(8,128)(2,1)} %collective-permute-done, bf16[4096,2,512]{2,0,1:T(8,128)(2,1)} %bitcast.214, bf16[192,2,512]{2,1,0:T(2,128)(2,1)S(1)} %reshape_reshape.19), kind=kOutput, calls=%fused_computation.35 | convolution fusion | flops 1614544896 | bytes 11927552 | tf_op jit(solution)/shard_map/tgk,gekn->ten/dot_general | solution.py:207
  173.4 1.1 dynamic-slice_bitcast_fusion.1
  174.5 1.5 collective-permute-start.1
  175.9 6.7 %add_convert_fusion = bf16[192,4096]{1,0:T(8,128)(2,1)S(1)} fusion(bf16[192,4096]{1,0:T(8,128)(2,1)} %collective-permute-done.2, bf16[4096,2,512]{2,0,1:T(8,128)(2,1)} %bitcast.215, bf16[192,2,512]{2,1,0:T(2,128)(2,1)S(1)} %reshape_reshape.22), kind=kOutput, calls=%fused_computation.34 | convolution fusion | flops 1614544896 | bytes 11927552 | tf_op jit(solution)/shard_map/tgk,gekn->ten/dot_general | solution.py:207
  182.6 1.1 copy-done.19
  183.8 0.9 dynamic-slice_bitcast_fusion
  184.7 0.6 collective-permute-start.3
  185.3 0.1 convolution_convert_fusion.2
  185.4 9.6 %collective-permute-done.1 = bf16[96,4096]{1,0:T(8,128)(2,1)S(1)} collective-permute-done((bf16[96,4096]{1,0:T(8,128)(2,1)}, bf16[96,4096]{1,0:T(8,128)(2,1)S(1)}, u32[]{:S(2)}, u32[]{:S(2)}) %collective-permute-start.1) | collective-permute-done | bytes 786464 | tf_op jit(solution)/shard_map/ppermute | solution.py:231
  195.1 15.9 %collective-permute-done.3 = bf16[96,4096]{1,0:T(8,128)(2,1)S(1)} collective-permute-done((bf16[96,4096]{1,0:T(8,128)(2,1)}, bf16[96,4096]{1,0:T(8,128)(2,1)S(1)}, u32[]{:S(2)}, u32[]{:S(2)}) %collective-permute-start.3) | collective-permute-done | bytes 786464 | tf_op jit(solution)/shard_map/ppermute | solution.py:231
  211.0 2.5 multiply_reduce_fusion.1
  213.5 1.9 multiply_convert_fusion.1
  215.4 0.9 copy-done.14
  216.3 2.5 convolution_convert_fusion
  218.8 3.8 all-to-all-start.2
  222.7 0.1 convolution_convert_fusion.3
  222.8 2.4 convolution_convert_fusion.1
  225.2 56.4 %all-to-all-done.2.rows_ref = bf16[8,36,4096]{2,1,0:T(8,128)(2,1)S(1)} async-done(((bf16[8,36,4096]{2,1,0:T(8,128)(2,1)}), bf16[8,36,4096]{2,1,0:T(8,128)(2,1)S(1)}, u32[]{:S(2)}, u32[]{:S(2)}) %all-to-all-start.2) | async-done | bytes 2359328 | tf_op jit(solution)/shard_map/all_to_all | solution.py:260
  281.6 4.4 all-to-all-start
  286.0 1.9 copy-done.3
  287.9 17.2 %shard_map.119 = bf16[8,36,4096]{2,1,0:T(8,128)(2,1)S(1)} custom-call(bf16[8,36,4096]{2,1,0:T(8,128)(2,1)S(1)} %all-to-all-done.2.rows_ref, bf16[4096,384]{1,0:T(8,128)(2,1)S(1)} %bitcast.209, bf16[4096,384]{1,0:T(8,128)(2,1)} %bitcast.228, bf16[384,4096]{1,0:T(8,128)(2,1)} %bitcast.230), custom_call_target="tpu_custom_call" | custom-call | flops 5435817984 | bytes 23592960 | tf_op jit(solution)/shard_map/pallas_call | solution.py:145
  305.1 1.5 copy-done.2
  306.7 38.3 %all-to-all-done.rows_ref = bf16[8,36,4096]{2,1,0:T(8,128)(2,1)} async-done(((bf16[8,36,4096]{2,1,0:T(8,128)(2,1)}), bf16[8,36,4096]{2,1,0:T(8,128)(2,1)}, u32[]{:S(2)}, u32[]{:S(2)}) %all-to-all-start) | async-done | bytes 2359328 | tf_op jit(solution)/shard_map/all_to_all | solution.py:260
  345.0 4.8 all-to-all-start.3
  349.8 19.5 %shard_map.118 = bf16[8,36,4096]{2,1,0:T(8,128)(2,1)} custom-call(bf16[8,36,4096]{2,1,0:T(8,128)(2,1)} %all-to-all-done.rows_ref, bf16[4096,384]{1,0:T(8,128)(2,1)S(1)} %bitcast.210, bf16[4096,384]{1,0:T(8,128)(2,1)} %bitcast.229, bf16[384,4096]{1,0:T(8,128)(2,1)} %bitcast.231), custom_call_target="tpu_custom_call" | custom-call | flops 5435817984 | bytes 23592960 | tf_op jit(solution)/shard_map/pallas_call | solution.py:145
  369.4 39.4 %all-to-all-done.3 = bf16[8,36,4096]{2,1,0:T(8,128)(2,1)} async-done(((bf16[8,36,4096]{2,1,0:T(8,128)(2,1)}), bf16[8,36,4096]{2,1,0:T(8,128)(2,1)}, u32[]{:S(2)}, u32[]{:S(2)}) %all-to-all-start.3) | async-done | bytes 2359328 | tf_op jit(solution)/shard_map/all_to_all | solution.py:262
  408.8 4.6 all-to-all-start.1
  413.4 0.3 fusion.137
  413.8 0.3 fusion.136
  414.2 2.6 convolution_bitcast_fusion.4
  416.9 0.2 copy-done.21
  417.1 3.6 fusion.15
  420.7 51.6 %all-to-all-done.1 = bf16[8,36,4096]{2,1,0:T(8,128)(2,1)} async-done(((bf16[8,36,4096]{2,1,0:T(8,128)(2,1)}), bf16[8,36,4096]{2,1,0:T(8,128)(2,1)}, u32[]{:S(2)}, u32[]{:S(2)}) %all-to-all-start.1) | async-done | bytes 2359328 | tf_op jit(solution)/shard_map/all_to_all | solution.py:262
  472.4 2.6 convolution_bitcast_fusion.6
  475.0 2.8 fusion.14
  477.8 1.3 maximum_bitcast_fusion
  (75 shorter events, 0.5 us)
Async XLA Ops:
  6.5 1.6 copy-start
  6.5 130.6 %all-gather.3.cloned.1.call-start = ((), (), s32[]{:S(2)}) async-start(), calls=%async_computation.4 | async-start | bytes 9437184 | tf_op jit(solution)/shard_map/all_gather | solution.py:198
  10.7 0.7 copy-start.27
  10.7 0.9 copy-start.24
  10.7 0.9 copy-start.25
  148.8 7.6 %copy-start.29 = (f32[8,384,384]{1,2,0:T(8,128)S(1)}, f32[8,384,384]{1,2,0:T(8,128)}, u32[]{:S(2)}) copy-start(f32[8,384,384]{1,2,0:T(8,128)} %get-tuple-element.26) | copy-start | bytes 14155780
  156.3 10.4 %collective-permute-start = (bf16[192,4096]{1,0:T(8,128)(2,1)}, bf16[192,4096]{1,0:T(8,128)(2,1)}, u32[]{:S(2)}, u32[]{:S(2)}) collective-permute-start(bf16[192,4096]{1,0:T(8,128)(2,1)} %fusion.4), channel_id=1, source_target_pairs={{0,1},{1,0},{2,3},{3,2},{4,5},{5,4},{6,7},{7,6},{8,9},{9,8},{10,11... | collective-permute-start | bytes 4718600 | tf_op jit(solution)/shard_map/ppermute | solution.py:224
  165.6 10.3 %collective-permute-start.2 = (bf16[192,4096]{1,0:T(8,128)(2,1)}, bf16[192,4096]{1,0:T(8,128)(2,1)}, u32[]{:S(2)}, u32[]{:S(2)}) collective-permute-start(bf16[192,4096]{1,0:T(8,128)(2,1)} %fusion.7), channel_id=1, source_target_pairs={{0,1},{1,0},{2,3},{3,2},{4,5},{5,4},{6,7},{7,6},{8,9},{9,8},{10,11... | collective-permute-start | bytes 4718600 | tf_op jit(solution)/shard_map/ppermute | solution.py:224
  173.4 9.2 %copy-start.16 = (bf16[192,4096]{1,0:T(8,128)(2,1)}, bf16[192,4096]{1,0:T(8,128)(2,1)S(1)}, u32[]{:S(2)}) copy-start(bf16[192,4096]{1,0:T(8,128)(2,1)S(1)} %add_convert_fusion.1) | copy-start | bytes 4718596
  174.5 20.6 %collective-permute-start.1 = (bf16[96,4096]{1,0:T(8,128)(2,1)}, bf16[96,4096]{1,0:T(8,128)(2,1)S(1)}, u32[]{:S(2)}, u32[]{:S(2)}) collective-permute-start(bf16[96,4096]{1,0:T(8,128)(2,1)} %dynamic-slice_bitcast_fusion.1), channel_id=1, source_target_pairs={{0,2},{2,0},{1,3},{3,1},{4,6},{6,4},{5,7},{7,5},{8,10},{10,8},{9,1... | collective-permute-start | bytes 2359304 | tf_op jit(solution)/shard_map/ppermute | solution.py:231
  182.6 1.2 copy-start.19
  182.6 2.7 copy-start.28
  182.6 28.4 %copy-start.5 = (bf16[2,1,96,4096]{3,2,1,0:T(8,128)(2,1)S(1)}, bf16[2,1,96,4096]{3,2,1,0:T(8,128)(2,1)}, u32[]{:S(2)}) copy-start(bf16[2,1,96,4096]{3,2,1,0:T(8,128)(2,1)} %param.12) | copy-start | bytes 4718596
  184.7 26.3 %collective-permute-start.3 = (bf16[96,4096]{1,0:T(8,128)(2,1)}, bf16[96,4096]{1,0:T(8,128)(2,1)S(1)}, u32[]{:S(2)}, u32[]{:S(2)}) collective-permute-start(bf16[96,4096]{1,0:T(8,128)(2,1)} %dynamic-slice_bitcast_fusion), channel_id=1, source_target_pairs={{0,2},{2,0},{1,3},{3,1},{4,6},{6,4},{5,7},{7,5},{8,10},{10,8},{9,1... | collective-permute-start | bytes 2359304 | tf_op jit(solution)/shard_map/ppermute | solution.py:231
  185.4 28.1 %copy-start.17 = (bf16[192,4096]{1,0:T(8,128)(2,1)S(1)}, bf16[192,4096]{1,0:T(8,128)(2,1)}, u32[]{:S(2)}) copy-start(bf16[192,4096]{1,0:T(8,128)(2,1)} %copy-done.16) | copy-start | bytes 4718596
  185.4 28.1 %copy-start.20 = (bf16[192,4096]{1,0:T(8,128)(2,1)S(1)}, bf16[192,4096]{1,0:T(8,128)(2,1)}, u32[]{:S(2)}) copy-start(bf16[192,4096]{1,0:T(8,128)(2,1)} %copy-done.19) | copy-start | bytes 4718596
  185.4 28.1 %copy-start.26 = (f32[4096]{0:T(1024)S(1)}, f32[4096]{0:T(1024)}, u32[]{:S(2)}) copy-start(f32[4096]{0:T(1024)} %param.18) | copy-start | bytes 49156
  195.1 18.4 %copy-start.8 = (bf16[96,4096]{1,0:T(8,128)(2,1)}, bf16[96,4096]{1,0:T(8,128)(2,1)S(1)}, u32[]{:S(2)}) copy-start(bf16[96,4096]{1,0:T(8,128)(2,1)S(1)} %collective-permute-done.1) | copy-start | bytes 2359300
  211.0 2.5 copy-start.10
  215.4 0.9 copy-start.14
  218.8 4.0 copy-start.12
  218.8 62.8 %all-to-all-start.2 = ((bf16[8,36,4096]{2,1,0:T(8,128)(2,1)}), bf16[8,36,4096]{2,1,0:T(8,128)(2,1)S(1)}, u32[]{:S(2)}, u32[]{:S(2)}) async-start(bf16[8,36,4096]{2,1,0:T(8,128)(2,1)} %convolution_convert_fusion), calls=%async_computation.2 | async-start | bytes 5242880 | tf_op jit(solution)/shard_map/all_to_all | solution.py:260
  281.6 63.4 %all-to-all-start = ((bf16[8,36,4096]{2,1,0:T(8,128)(2,1)}), bf16[8,36,4096]{2,1,0:T(8,128)(2,1)}, u32[]{:S(2)}, u32[]{:S(2)}) async-start(bf16[8,36,4096]{2,1,0:T(8,128)(2,1)} %convolution_convert_fusion.1), calls=%async_computation | async-start | bytes 5242880 | tf_op jit(solution)/shard_map/all_to_all | solution.py:260
  286.0 1.9 copy-start.3
  305.1 1.6 copy-start.2
  306.7 43.1 %copy-start.4 = (bf16[1,4096,384]{2,1,0:T(8,128)(2,1)S(1)}, bf16[1,4096,384]{2,1,0:T(8,128)(2,1)}, u32[]{:S(2)}) copy-start(bf16[1,4096,384]{2,1,0:T(8,128)(2,1)} %param.21) | copy-start | bytes 9437188
  345.0 63.8 %all-to-all-start.3 = ((bf16[8,36,4096]{2,1,0:T(8,128)(2,1)}), bf16[8,36,4096]{2,1,0:T(8,128)(2,1)}, u32[]{:S(2)}, u32[]{:S(2)}) async-start(bf16[8,36,4096]{2,1,0:T(8,128)(2,1)} %copy-done.2), calls=%async_computation.3 | async-start | bytes 5242880 | tf_op jit(solution)/shard_map/all_to_all | solution.py:262
  369.3 44.1 %copy-start.15 = (bf16[96,4096]{1,0:T(8,128)(2,1)S(1)}, bf16[96,4096]{1,0:T(8,128)(2,1)}, u32[]{:S(2)}) copy-start(bf16[96,4096]{1,0:T(8,128)(2,1)} %copy-done.14) | copy-start | bytes 2359300
  369.3 44.1 %copy-start.23 = (bf16[4096,8]{0,1:T(8,128)(2,1)S(1)}, bf16[4096,8]{0,1:T(8,128)(2,1)}, u32[]{:S(2)}) copy-start(bf16[4096,8]{0,1:T(8,128)(2,1)} %param.19) | copy-start | bytes 196612
  369.3 44.4 %copy-start.13 = (bf16[96,4096]{1,0:T(8,128)(2,1)S(1)}, bf16[96,4096]{1,0:T(8,128)(2,1)}, u32[]{:S(2)}) copy-start(bf16[96,4096]{1,0:T(8,128)(2,1)} %get-tuple-element.9) | copy-start | bytes 2359300
  408.8 63.6 %all-to-all-start.1 = ((bf16[8,36,4096]{2,1,0:T(8,128)(2,1)}), bf16[8,36,4096]{2,1,0:T(8,128)(2,1)}, u32[]{:S(2)}, u32[]{:S(2)}) async-start(bf16[8,36,4096]{2,1,0:T(8,128)(2,1)} %shard_map.118), calls=%async_computation.1 | async-start | bytes 5242880 | tf_op jit(solution)/shard_map/all_to_all | solution.py:262
  414.2 2.6 copy-start.6
  414.2 2.6 copy-start.11
  414.2 2.9 copy-start.21
  420.7 54.2 %copy-start.9 = (bf16[96,4096]{1,0:T(8,128)(2,1)S(1)}, bf16[96,4096]{1,0:T(8,128)(2,1)}, u32[]{:S(2)}) copy-start(bf16[96,4096]{1,0:T(8,128)(2,1)} %copy-done.8) | copy-start | bytes 2359300
  472.4 2.6 copy-start.7
  472.4 2.7 copy-start.18
  475.0 2.8 copy-start.22
  475.0 4.1 copy-start.1
Sparse Core Ops, SparseCore 0:
  9.5 127.6 all-gather.2

commit v3 on v2

--- a/solution.py
+++ b/solution.py
@@ -160,6 +160,110 @@
     return result.reshape(given)
 
 
+def gather_kernel(n_line, n_subs, own_ref, out_ref, local_sem, right_send, left_send, line_recv, y_send, y_recv):
+    place = lax.axis_index("expert")
+    group = lax.axis_index("group")
+    rows, columns = own_ref.shape
+    half = rows // 2
+    sub_rows = half // n_subs
+    mesh_ids = pl.DeviceIdType.MESH
+    right, left = {"expert": place + 1}, {"expert": place - 1}
+    other = {"group": 1 - group}
+    has_right, has_left = place < n_line - 1, place > 0
+    barrier = pltpu.get_barrier_semaphore()
+    pl.semaphore_signal(barrier, inc=1, device_id=other, device_id_type=mesh_ids)
+
+    @pl.when(has_right)
+    def _():
+        pl.semaphore_signal(barrier, inc=1, device_id=right, device_id_type=mesh_ids)
+
+    @pl.when(has_left)
+    def _():
+        pl.semaphore_signal(barrier, inc=1, device_id=left, device_id_type=mesh_ids)
+
+    peers = 1 + jnp.where(has_right, 1, 0) + jnp.where(has_left, 1, 0)
+    pl.semaphore_wait(barrier, peers)
+
+    def spot(side, origin, sub):
+        start = pl.multiple_of(side * half + sub * sub_rows, sub_rows)
+        return out_ref.at[
+            pl.ds(start, sub_rows), pl.ds(pl.multiple_of(origin * columns, columns), columns)
+        ]
+
+    def along(origin, sub, target, send_sem, from_own):
+        source = spot(group, origin, sub)
+        if from_own:
+            start = pl.multiple_of(group * half + sub * sub_rows, sub_rows)
+            source = own_ref.at[pl.ds(start, sub_rows)]
+        return pltpu.make_async_remote_copy(
+            src_ref=source,
+            dst_ref=spot(group, origin, sub),
+            send_sem=send_sem.at[origin, sub],
+            recv_sem=line_recv.at[origin, sub],
+            device_id=target,
+            device_id_type=mesh_ids,
+        )
+
+    def across(side, origin, sub):
+        return pltpu.make_async_remote_copy(
+            src_ref=spot(side, origin, sub),
+            dst_ref=spot(side, origin, sub),
+            send_sem=y_send.at[origin, sub],
+            recv_sem=y_recv.at[origin, sub],
+            device_id=other,
+            device_id_type=mesh_ids,
+        )
+
+    for sub in range(n_subs):
+        pl.when(has_right)(lambda sub=sub: along(place, sub, right, right_send, True).start())
+        pl.when(has_left)(lambda sub=sub: along(place, sub, left, left_send, True).start())
+    own_place = out_ref.at[:, pl.ds(pl.multiple_of(place * columns, columns), columns)]
+    keep = pltpu.make_async_copy(own_ref, own_place, local_sem)
+    keep.start()
+
+    def pass_on(origin, sub, onward, target, send_sem):
+        along(origin, sub, target, send_sem, False).wait_recv()
+        pl.when(onward)(lambda: along(origin, sub, target, send_sem, False).start())
+        across(group, origin, sub).start()
+
+    def finish(origin, sub, onward, target, send_sem):
+        pl.when(onward)(lambda: along(origin, sub, target, send_sem, False).wait_send())
+        across(group, origin, sub).wait_send()
+        across(1 - group, origin, sub).wait_recv()
+
+    for act in (pass_on, finish):
+        for distance in range(1, n_line):
+            for sub in range(n_subs):
+                pl.when(place >= distance)(
+                    lambda: act(place - distance, sub, has_right, right, right_send)
+                )
+                pl.when(place + distance < n_line)(
+                    lambda: act(place + distance, sub, has_left, left, left_send)
+                )
+    for sub in range(n_subs):
+        pl.when(has_right)(lambda sub=sub: along(place, sub, right, right_send, True).wait_send())
+        pl.when(has_left)(lambda sub=sub: along(place, sub, left, left_send, True).wait_send())
+    keep.wait()
+
+
+def gather_projection(out_proj):
+    n_line = lax.axis_size("expert")
+    rows, columns = out_proj.shape
+    n_subs = 2
+    sems = pltpu.SemaphoreType.DMA((n_line, n_subs))
+    return pl.pallas_call(
+        functools.partial(gather_kernel, n_line, n_subs),
+        out_shape=jax.ShapeDtypeStruct((rows, columns * n_line), jnp.bfloat16),
+        in_specs=[pl.BlockSpec(memory_space=pl.ANY)],
+        out_specs=pl.BlockSpec(memory_space=pl.ANY),
+        scratch_shapes=[pltpu.SemaphoreType.DMA] + [sems] * 5,
+        compiler_params=pltpu.CompilerParams(collective_id=1, has_side_effects=True),
+        cost_estimate=pl.CostEstimate(
+            flops=0, bytes_accessed=4 * rows * columns * n_line, transcendentals=0
+        ),
+    )(out_proj)
+
+
 def local(
     stream,
     queries,
@@ -177,10 +281,8 @@
     f32 = jnp.float32
     bf16 = jnp.bfloat16
     tensor_index = lax.axis_index(TENSOR)
-    group_index = lax.axis_index("group")
     core_index = lax.axis_index("core")
     x_index = lax.axis_index("x")
-    n_groups = lax.axis_size("group")
     n_x = lax.axis_size("x")
     micros = stream.shape[0]
     heads_here = queries.shape[-1] // HD
@@ -192,21 +294,14 @@
     gate_w = gate_proj[0]
     up_w = up_proj[0]
     down_w = down_proj[0]
-    proj_rows, proj_cols = out_proj.shape
-    piece_rows = proj_rows // n_groups
-    piece = lax.dynamic_slice_in_dim(out_proj, group_index * piece_rows, piece_rows, 0)
-    pieces = lax.all_gather(piece, ("group", "expert"), axis=0, tiled=False)
-    pieces = pieces.reshape(n_groups, -1, piece_rows, proj_cols)
+    proj_full = gather_projection(out_proj)
     kv_width = key_rows.shape[-1]
     kv_all = lax.all_gather(
         jnp.concatenate([key_rows[:, 0], value_rows[:, 0]], axis=-1), TENSOR, axis=1, tiled=True
     )
 
     def project(rows):
-        split_rows = rows.reshape(rows.shape[0], n_groups, piece_rows)
-        return jnp.einsum(
-            "tgk,gekn->ten", split_rows, pieces, preferred_element_type=f32
-        ).reshape(rows.shape[0], model_width).astype(bf16)
+        return jnp.dot(rows, proj_full, preferred_element_type=f32).astype(bf16)
 
     results = []
     for micro in range(micros):

time: 493 us -> 444 us (0.901)
  waiting for transfers between devices: 314 us -> 213 us
  Pallas kernels: 36.7 us -> 122 us
  local copies, waits for them, and re-layouts: 27.8 us -> 14.3 us
  between operations: 14.1 us -> 0.65 us
  matrix products: 57.4 us -> 52.4 us
    all_gather x1 -> x0, waiting for transfers between devices: 102 us -> none  [local(): pieces = lax.all_gather(piece, ('group', 'expert'), axis=0, tiled=False)]
    pallas_call x0 -> x1, Pallas kernels: none -> 85.7 us  [gather_projection(): pl.pallas_call(functools.partial(gather_kernel, n_line, n_subs), out_shap...]
    reshape x1 -> x0, local copies, waits for them, and re-layouts: 11.6 us -> none  [local(): pieces = pieces.reshape(n_groups, -1, piece_rows, proj_cols)]
  transfers between devices with their start and end apart: 9 -> 8, of which waited for: 7 -> 6; matrix products, arithmetic and copies ran while one was open for 10% -> 9% of each run, Pallas kernels for 8% -> 8%
where the time goes in v3:
time: 444 us; the launch traced here: 439 us
  waiting for transfers between devices  213 us (48%)
  Pallas kernels  122 us (27%)
  matrix products  52.4 us (12%)
  starting transfers between devices  19.4 us (4%)
  local copies, waits for them, and re-layouts  14.3 us (3%)
  blocking collectives  10 us (2%)
  other arithmetic  7.19 us (2%)
    all_to_all x2, waiting for transfers between devices, local(): lax.all_to_all(packed, CHIPS, split_axis=0, concat_axis=0, tiled=True)  95.2 us
    all_to_all x2, waiting for transfers between devices, local(): lax.all_to_all(summed, CHIPS, split_axis=0, concat_axis=0, tiled=True)  90.7 us
    pallas_call x1, Pallas kernels, gather_projection(): pl.pallas_call(functools.partial(gather_kernel, n_line, n_subs), out_shap...  85.7 us
    pallas_call x2, Pallas kernels, run_experts(): pl.pallas_call(functools.partial(experts_kernel, n_chunks), out_shape=jax...  36.7 us
    ppermute x2, waiting for transfers between devices, local(): attn_out = here.astype(f32) + lax.ppermute(away, 'x', SWAP).astype(f32)  27.1 us
    dot_general x4, matrix products, project(): return jnp.dot(rows, proj_full, preferred_element_type=f32).astype(bf16)  23.9 us
    all_gather x1, blocking collectives, local(): lax.all_gather(jnp.concatenate([key_rows[:, 0], value_rows[:, 0]], axis=-...  10 us
  transfers between devices with their start and end apart: 8, of which 6 were waited for; matrix products, arithmetic and copies ran while one was open for 9% of the time, Pallas kernels for 8%

profile of v3, /device:TPU:0, one launch (start us, length us, event | category | flops | bytes accessed | tf_op | source)
XLA Modules:
  0.0 439.4 jit_solution(7827578914353754789)
XLA Ops:
  0.0 0.8 slice_reduce_fusion.1
  0.8 1.0 pad_maximum_fusion
  1.8 10.0 %all_gather.3 = bf16[2,384,512]{2,1,0:T(8,128)(2,1)S(1)} all-gather(bf16[2,96,512]{2,1,0:T(8,128)(2,1)S(1)} %pad_maximum_fusion), channel_id=1, replica_groups=mesh['group'=2,'expert'=4,'x'=2,'core'=2] {'x','core'}, dimensions={1}, use_global_device_ids=true | all-gather | bytes 983040 | tf_op jit(solution)/shard_map/all_gather | solution.py:299
  11.8 0.8 fusion.113
  12.7 0.1 fusion.112
  12.8 0.4 copy.52
  13.2 0.2 fusion.30
  13.4 0.3 copy-done.24
  13.7 4.1 fusion.114
  17.8 2.9 fusion.26
  20.7 0.5 copy.41
  21.3 0.3 reshape_reshape.6
  21.6 85.7 %shard_map.118 = bf16[1024,4096]{1,0:T(8,128)(2,1)} custom-call(bf16[1024,1024]{1,0:T(8,128)(2,1)} %own_ref.1), custom_call_target="tpu_custom_call" | custom-call | bytes 16777216 | tf_op jit(solution)/shard_map/pallas_call | solution.py:254
  107.3 0.1 constant_dynamic-slice_fusion.2
  107.4 6.3 %convolution_convert_fusion.4 = bf16[192,4096]{1,0:T(8,128)(2,1)} fusion(bf16[192,1024]{1,0:T(8,128)(2,1)S(1)} %bitcast.196, bf16[1024,4096]{1,0:T(8,128)(2,1)} %shard_map.118), kind=kOutput, calls=%fused_computation.7 | convolution fusion | flops 1611399168 | bytes 10354688 | tf_op jit(solution)/shard_map/dot_general | solution.py:304
  113.8 0.4 copy.53
  114.1 0.6 copy-done.22
  114.7 4.1 fusion.119
  118.8 3.0 fusion.27
  121.7 0.5 copy.46
  122.3 0.3 reshape_reshape.7
  122.6 0.1 constant_dynamic-slice_fusion
  122.7 6.3 %convolution_convert_fusion.2 = bf16[192,4096]{1,0:T(8,128)(2,1)} fusion(bf16[192,1024]{1,0:T(8,128)(2,1)S(1)} %bitcast.195, bf16[1024,4096]{1,0:T(8,128)(2,1)} %shard_map.118), kind=kOutput, calls=%fused_computation.4 | convolution fusion | flops 1611399168 | bytes 10354688 | tf_op jit(solution)/shard_map/dot_general | solution.py:304
  129.0 5.6 %add_convert_fusion.1 = bf16[192,4096]{1,0:T(8,128)(2,1)S(1)} fusion(bf16[192,4096]{1,0:T(8,128)(2,1)} %collective-permute-done, bf16[192,1024]{1,0:T(8,128)(2,1)S(1)} %bitcast.193, bf16[1024,4096]{1,0:T(8,128)(2,1)} %shard_map.118), kind=kOutput, calls=%fused_computation.31 | convolution fusion | flops 1614544896 | bytes 11927552 | tf_op jit(solution)/shard_map/dot_general | solution.py:304
  134.6 0.0 copy-start.14
  134.6 1.0 dynamic-slice_bitcast_fusion.1
  135.7 1.1 collective-permute-start.1
  136.8 5.6 %add_convert_fusion = bf16[192,4096]{1,0:T(8,128)(2,1)S(1)} fusion(bf16[192,4096]{1,0:T(8,128)(2,1)} %collective-permute-done.2, bf16[192,1024]{1,0:T(8,128)(2,1)S(1)} %bitcast.194, bf16[1024,4096]{1,0:T(8,128)(2,1)} %shard_map.118), kind=kOutput, calls=%fused_computation.30 | convolution fusion | flops 1614544896 | bytes 11927552 | tf_op jit(solution)/shard_map/dot_general | solution.py:304
  142.4 0.0 copy-start.26
  142.4 1.1 copy-done.17
  143.5 0.9 dynamic-slice_bitcast_fusion
  144.5 0.9 collective-permute-start.3
  145.4 0.1 convolution_convert_fusion.6
  145.6 10.6 %collective-permute-done.1 = bf16[96,4096]{1,0:T(8,128)(2,1)S(1)} collective-permute-done((bf16[96,4096]{1,0:T(8,128)(2,1)}, bf16[96,4096]{1,0:T(8,128)(2,1)S(1)}, u32[]{:S(2)}, u32[]{:S(2)}) %collective-permute-start.1) | collective-permute-done | bytes 786464 | tf_op jit(solution)/shard_map/ppermute | solution.py:326
  156.2 16.5 %collective-permute-done.3 = bf16[96,4096]{1,0:T(8,128)(2,1)S(1)} collective-permute-done((bf16[96,4096]{1,0:T(8,128)(2,1)}, bf16[96,4096]{1,0:T(8,128)(2,1)S(1)}, u32[]{:S(2)}, u32[]{:S(2)}) %collective-permute-start.3) | collective-permute-done | bytes 786464 | tf_op jit(solution)/shard_map/ppermute | solution.py:326
  172.7 2.5 multiply_reduce_fusion.1
  175.2 2.1 multiply_convert_fusion.1
  177.3 0.9 copy-done.11
  178.2 2.4 convolution_convert_fusion
  180.6 4.4 all-to-all-start.2
  185.0 0.1 convolution_convert_fusion.7
  185.1 2.4 convolution_convert_fusion.1
  187.5 56.8 %all-to-all-done.2.rows_ref = bf16[8,36,4096]{2,1,0:T(8,128)(2,1)S(1)} async-done(((bf16[8,36,4096]{2,1,0:T(8,128)(2,1)}), bf16[8,36,4096]{2,1,0:T(8,128)(2,1)S(1)}, u32[]{:S(2)}, u32[]{:S(2)}) %all-to-all-start.2) | async-done | bytes 2359328 | tf_op jit(solution)/shard_map/all_to_all | solution.py:355
  244.3 4.4 %all-to-all-start = ((bf16[8,36,4096]{2,1,0:T(8,128)(2,1)}), bf16[8,36,4096]{2,1,0:T(8,128)(2,1)}, u32[]{:S(2)}, u32[]{:S(2)}) async-start(bf16[8,36,4096]{2,1,0:T(8,128)(2,1)} %convolution_convert_fusion.1), calls=%async_computation | async-start | bytes 5242880 | tf_op jit(solution)/shard_map/all_to_all | solution.py:355
  248.7 1.9 copy-done.2
  250.6 17.2 %shard_map.120 = bf16[8,36,4096]{2,1,0:T(8,128)(2,1)S(1)} custom-call(bf16[8,36,4096]{2,1,0:T(8,128)(2,1)S(1)} %all-to-all-done.2.rows_ref, bf16[4096,384]{1,0:T(8,128)(2,1)S(1)} %bitcast.181, bf16[4096,384]{1,0:T(8,128)(2,1)} %bitcast.199, bf16[384,4096]{1,0:T(8,128)(2,1)} %bitcast.201), custom_call_target="tpu_custom_call" | custom-call | flops 5435817984 | bytes 23592960 | tf_op jit(solution)/shard_map/pallas_call | solution.py:145
  267.8 1.5 copy-done.1
  269.4 38.3 %all-to-all-done.rows_ref = bf16[8,36,4096]{2,1,0:T(8,128)(2,1)} async-done(((bf16[8,36,4096]{2,1,0:T(8,128)(2,1)}), bf16[8,36,4096]{2,1,0:T(8,128)(2,1)}, u32[]{:S(2)}, u32[]{:S(2)}) %all-to-all-start) | async-done | bytes 2359328 | tf_op jit(solution)/shard_map/all_to_all | solution.py:355
  307.7 4.8 %all-to-all-start.3 = ((bf16[8,36,4096]{2,1,0:T(8,128)(2,1)}), bf16[8,36,4096]{2,1,0:T(8,128)(2,1)}, u32[]{:S(2)}, u32[]{:S(2)}) async-start(bf16[8,36,4096]{2,1,0:T(8,128)(2,1)} %copy-done.1), calls=%async_computation.3 | async-start | bytes 5242880 | tf_op jit(solution)/shard_map/all_to_all | solution.py:357
  312.5 19.5 %shard_map.119 = bf16[8,36,4096]{2,1,0:T(8,128)(2,1)} custom-call(bf16[8,36,4096]{2,1,0:T(8,128)(2,1)} %all-to-all-done.rows_ref, bf16[4096,384]{1,0:T(8,128)(2,1)S(1)} %bitcast.182, bf16[4096,384]{1,0:T(8,128)(2,1)} %bitcast.200, bf16[384,4096]{1,0:T(8,128)(2,1)} %bitcast.202), custom_call_target="tpu_custom_call" | custom-call | flops 5435817984 | bytes 23592960 | tf_op jit(solution)/shard_map/pallas_call | solution.py:145
  332.0 39.5 %all-to-all-done.3 = bf16[8,36,4096]{2,1,0:T(8,128)(2,1)} async-done(((bf16[8,36,4096]{2,1,0:T(8,128)(2,1)}), bf16[8,36,4096]{2,1,0:T(8,128)(2,1)}, u32[]{:S(2)}, u32[]{:S(2)}) %all-to-all-start.3) | async-done | bytes 2359328 | tf_op jit(solution)/shard_map/all_to_all | solution.py:357
  371.5 3.8 all-to-all-start.1
  375.4 1.4 fusion.124
  376.9 0.3 fusion.125
  377.3 2.6 convolution_bitcast_fusion
  380.0 0.2 copy-done.19
  380.2 3.6 fusion.11
  383.8 51.2 %all-to-all-done.1 = bf16[8,36,4096]{2,1,0:T(8,128)(2,1)S(1)} async-done(((bf16[8,36,4096]{2,1,0:T(8,128)(2,1)}), bf16[8,36,4096]{2,1,0:T(8,128)(2,1)S(1)}, u32[]{:S(2)}, u32[]{:S(2)}) %all-to-all-start.1) | async-done | bytes 2359328 | tf_op jit(solution)/shard_map/all_to_all | solution.py:357
  434.9 0.7 convolution_bitcast_fusion.2
  435.7 0.7 copy-done.6
  436.4 0.5 copy-done.16
  436.8 0.9 fusion.10
  437.7 0.2 copy-done.20
  438.0 1.3 maximum_bitcast_fusion
  (61 shorter events, 0.3 us)
Async XLA Ops:
  0.0 375.3 %copy-start = (bf16[4096,8]{0,1:T(8,128)(2,1)S(1)}, bf16[4096,8]{0,1:T(8,128)(2,1)}, u32[]{:S(2)}) copy-start(bf16[4096,8]{0,1:T(8,128)(2,1)} %param.19) | copy-start | bytes 196612
  0.0 12.7 %copy-start.21 = (bf16[2,1,384,1024]{3,2,1,0:T(8,128)(2,1)S(1)}, bf16[2,1,384,1024]{3,2,1,0:T(8,128)(2,1)}, u32[]{:S(2)}) copy-start(bf16[2,1,384,1024]{3,2,1,0:T(8,128)(2,1)} %param.13) | copy-start | bytes 4718596
  12.8 0.9 copy-start.24
  13.7 4.1 copy-start.23
  113.8 0.9 copy-start.22
  113.8 15.3 %collective-permute-start = (bf16[192,4096]{1,0:T(8,128)(2,1)}, bf16[192,4096]{1,0:T(8,128)(2,1)}, u32[]{:S(2)}, u32[]{:S(2)}) collective-permute-start(bf16[192,4096]{1,0:T(8,128)(2,1)} %convolution_convert_fusion.4), channel_id=1, source_target_pairs={{0,1},{1,0},{2,3},{3,2},{4,5},{5,4},{6,7},{7,6},{8,9},{9,8},{10,11... | collective-permute-start | bytes 4718600 | tf_op jit(solution)/shard_map/ppermute | solution.py:319
  129.0 7.8 %collective-permute-start.2 = (bf16[192,4096]{1,0:T(8,128)(2,1)}, bf16[192,4096]{1,0:T(8,128)(2,1)}, u32[]{:S(2)}, u32[]{:S(2)}) collective-permute-start(bf16[192,4096]{1,0:T(8,128)(2,1)} %convolution_convert_fusion.2), channel_id=1, source_target_pairs={{0,1},{1,0},{2,3},{3,2},{4,5},{5,4},{6,7},{7,6},{8,9},{9,8},{10,11... | collective-permute-start | bytes 4718600 | tf_op jit(solution)/shard_map/ppermute | solution.py:319
  134.6 7.8 %copy-start.14 = (bf16[192,4096]{1,0:T(8,128)(2,1)}, bf16[192,4096]{1,0:T(8,128)(2,1)S(1)}, u32[]{:S(2)}) copy-start(bf16[192,4096]{1,0:T(8,128)(2,1)S(1)} %add_convert_fusion.1) | copy-start | bytes 4718596
  135.7 20.5 %collective-permute-start.1 = (bf16[96,4096]{1,0:T(8,128)(2,1)}, bf16[96,4096]{1,0:T(8,128)(2,1)S(1)}, u32[]{:S(2)}, u32[]{:S(2)}) collective-permute-start(bf16[96,4096]{1,0:T(8,128)(2,1)} %dynamic-slice_bitcast_fusion.1), channel_id=1, source_target_pairs={{0,2},{2,0},{1,3},{3,1},{4,6},{6,4},{5,7},{7,5},{8,10},{10,8},{9,1... | collective-permute-start | bytes 2359304 | tf_op jit(solution)/shard_map/ppermute | solution.py:326
  142.4 1.2 copy-start.17
  142.4 3.0 copy-start.26
  142.4 30.3 %copy-start.4 = (bf16[2,1,96,4096]{3,2,1,0:T(8,128)(2,1)S(1)}, bf16[2,1,96,4096]{3,2,1,0:T(8,128)(2,1)}, u32[]{:S(2)}) copy-start(bf16[2,1,96,4096]{3,2,1,0:T(8,128)(2,1)} %param.12) | copy-start | bytes 4718596
  144.5 28.2 %collective-permute-start.3 = (bf16[96,4096]{1,0:T(8,128)(2,1)}, bf16[96,4096]{1,0:T(8,128)(2,1)S(1)}, u32[]{:S(2)}, u32[]{:S(2)}) collective-permute-start(bf16[96,4096]{1,0:T(8,128)(2,1)} %dynamic-slice_bitcast_fusion), channel_id=1, source_target_pairs={{0,2},{2,0},{1,3},{3,1},{4,6},{6,4},{5,7},{7,5},{8,10},{10,8},{9,1... | collective-permute-start | bytes 2359304 | tf_op jit(solution)/shard_map/ppermute | solution.py:326
  145.6 29.6 %copy-start.15 = (bf16[192,4096]{1,0:T(8,128)(2,1)S(1)}, bf16[192,4096]{1,0:T(8,128)(2,1)}, u32[]{:S(2)}) copy-start(bf16[192,4096]{1,0:T(8,128)(2,1)} %copy-done.14) | copy-start | bytes 4718596
  145.6 29.6 %copy-start.18 = (bf16[192,4096]{1,0:T(8,128)(2,1)S(1)}, bf16[192,4096]{1,0:T(8,128)(2,1)}, u32[]{:S(2)}) copy-start(bf16[192,4096]{1,0:T(8,128)(2,1)} %copy-done.17) | copy-start | bytes 4718596
  145.6 29.7 %copy-start.25 = (f32[4096]{0:T(1024)S(1)}, f32[4096]{0:T(1024)}, u32[]{:S(2)}) copy-start(f32[4096]{0:T(1024)} %param.18) | copy-start | bytes 49156
  156.2 19.0 %copy-start.7 = (bf16[96,4096]{1,0:T(8,128)(2,1)}, bf16[96,4096]{1,0:T(8,128)(2,1)S(1)}, u32[]{:S(2)}) copy-start(bf16[96,4096]{1,0:T(8,128)(2,1)S(1)} %collective-permute-done.1) | copy-start | bytes 2359300
  172.7 2.5 copy-start.9
  177.3 0.9 copy-start.11
  180.6 4.5 %copy-start.13 = (bf16[96,4096]{1,0:T(8,128)(2,1)S(1)}, bf16[96,4096]{1,0:T(8,128)(2,1)}, u32[]{:S(2)}) copy-start(bf16[96,4096]{1,0:T(8,128)(2,1)} %get-tuple-element.9) | copy-start | bytes 2359300
  180.6 63.7 %all-to-all-start.2 = ((bf16[8,36,4096]{2,1,0:T(8,128)(2,1)}), bf16[8,36,4096]{2,1,0:T(8,128)(2,1)S(1)}, u32[]{:S(2)}, u32[]{:S(2)}) async-start(bf16[8,36,4096]{2,1,0:T(8,128)(2,1)} %convolution_convert_fusion), calls=%async_computation.2 | async-start | bytes 5242880 | tf_op jit(solution)/shard_map/all_to_all | solution.py:355
  244.3 63.4 %all-to-all-start = ((bf16[8,36,4096]{2,1,0:T(8,128)(2,1)}), bf16[8,36,4096]{2,1,0:T(8,128)(2,1)}, u32[]{:S(2)}, u32[]{:S(2)}) async-start(bf16[8,36,4096]{2,1,0:T(8,128)(2,1)} %convolution_convert_fusion.1), calls=%async_computation | async-start | bytes 5242880 | tf_op jit(solution)/shard_map/all_to_all | solution.py:355
  248.7 1.9 copy-start.2
  267.8 1.6 copy-start.1
  269.4 43.1 %copy-start.3 = (bf16[1,4096,384]{2,1,0:T(8,128)(2,1)S(1)}, bf16[1,4096,384]{2,1,0:T(8,128)(2,1)}, u32[]{:S(2)}) copy-start(bf16[1,4096,384]{2,1,0:T(8,128)(2,1)} %param.21) | copy-start | bytes 9437188
  307.7 63.8 %all-to-all-start.3 = ((bf16[8,36,4096]{2,1,0:T(8,128)(2,1)}), bf16[8,36,4096]{2,1,0:T(8,128)(2,1)}, u32[]{:S(2)}, u32[]{:S(2)}) async-start(bf16[8,36,4096]{2,1,0:T(8,128)(2,1)} %copy-done.1), calls=%async_computation.3 | async-start | bytes 5242880 | tf_op jit(solution)/shard_map/all_to_all | solution.py:357
  332.0 44.8 %copy-start.12 = (bf16[96,4096]{1,0:T(8,128)(2,1)S(1)}, bf16[96,4096]{1,0:T(8,128)(2,1)}, u32[]{:S(2)}) copy-start(bf16[96,4096]{1,0:T(8,128)(2,1)} %copy-done.11) | copy-start | bytes 2359300
  371.5 63.4 %all-to-all-start.1 = ((bf16[8,36,4096]{2,1,0:T(8,128)(2,1)}), bf16[8,36,4096]{2,1,0:T(8,128)(2,1)S(1)}, u32[]{:S(2)}, u32[]{:S(2)}) async-start(bf16[8,36,4096]{2,1,0:T(8,128)(2,1)} %shard_map.119), calls=%async_computation.1 | async-start | bytes 5242880 | tf_op jit(solution)/shard_map/all_to_all | solution.py:357
  377.3 2.6 copy-start.5
  377.3 2.6 copy-start.10
  377.3 2.9 copy-start.19
  383.8 51.9 %copy-start.8 = (bf16[96,4096]{1,0:T(8,128)(2,1)S(1)}, bf16[96,4096]{1,0:T(8,128)(2,1)}, u32[]{:S(2)}) copy-start(bf16[96,4096]{1,0:T(8,128)(2,1)} %copy-done.7) | copy-start | bytes 2359300
  434.9 1.4 copy-start.6
  434.9 1.9 copy-start.16
  436.8 1.1 copy-start.20
